TPU v7x, 32 devices: a whole 2x2x4 slice. The times are simulated.
32 devices in a mesh: parts: 2 (over y), region: 4 (over z), aux: 2 (over x), pno: 2 (over core).
Axes of the slice: x: 2, y: 2, z: 4, core: 2. Of those that a mesh axis runs over, the one named last changes fastest.
Arguments:
- three_index: bfloat16 [24, 3072, 256], P(('parts', 'region'), 'aux'), parts along dimension 0, may hold values from -1 to 1
- pno_maps: bfloat16 [128, 2, 256, 256], P(('parts', 'region'), None, None, 'pno'), parts along dimension 0, may hold values from -0.375 to 0.375
- amplitudes: bfloat16 [128, 256, 256], P(('parts', 'region'), 'pno'), parts along dimension 0, may hold values from -6 to 6
- pair_orbitals: int32 [128, 2], P('parts'), parts along dimension 0, may hold values from 0 to 11, as said below
- neighbours: int32 [128, 4], P(('parts', 'region')), parts along dimension 0, may hold values from 0 to 63, as said below
- couplings: float32 [128, 4], P(('parts', 'region')), parts along dimension 0, may hold values from -0.5 to 0.5
- pno_energies: float32 [128, 256], P(('parts', 'region')), parts along dimension 0, may hold values from 0.5 to 3
- occ_energies: float32 [24], P('parts'), parts along dimension 0, may hold values from -2 to -0.3
- pno_counts: int32 [128], P(('parts', 'region')), parts along dimension 0, may hold values from 64 to 256
Outputs:
- new_amplitudes: bfloat16 [128, 256, 256], P(('parts', 'region'), 'pno'), parts along dimension 0
- density: float32 [24, 256], P(('parts', 'region')), parts along dimension 0
There are 2 independent parts, one for each index of `parts`. A program takes and returns all parts, laid end to end along the dimension named above; each array names one. Nothing has to cross between parts.
Inputs may be any that keep to these rules, and one draw needn't show every extreme that they name: `pair_orbitals`: pair p belongs to region p // 16; orbital o lies in region o // 3; a pair's first orbital lies in its own region; of one region's pairs at most 8 have their second orbital in any one region, and exactly 8 in some region. The neighbours of pair p belong to regions p // 16 - 1 to p // 16 + 1.
All inputs are finite; a program needn't handle non-finite values.
Results may differ from a plain program's by a relative error of at most 0.0065.
Values may be sent and summed in bfloat16 or wider, within the bound.
A program may use at most 128 MiB of HBM per device.

v0:
```python
import jax
import jax.numpy as jnp
from jax import lax
from jax.sharding import PartitionSpec as P


def with_halo(block, sides, width):
    for axis, dim in sides:
        count = lax.axis_size(axis)
        forward = [(i, i + 1) for i in range(count - 1)]
        backward = [(target, source) for source, target in forward]
        low = lax.ppermute(
            lax.slice_in_dim(block, block.shape[dim] - width, None, axis=dim), axis, forward
        )
        high = lax.ppermute(lax.slice_in_dim(block, 0, width, axis=dim), axis, backward)
        block = jnp.concatenate([low, block, high], axis=dim)
    return block


def body(
    three_index,
    pno_maps,
    amplitudes,
    pair_orbitals,
    neighbours,
    couplings,
    pno_energies,
    occ_energies,
    pno_counts,
):
    regions = lax.axis_size("region")
    region_index = lax.axis_index("region")
    pno_index = lax.axis_index("pno")
    occ_dev, aux_rows, virtuals = three_index.shape
    pair_dev = pno_maps.shape[0]
    columns = pno_maps.shape[3]
    width = amplitudes.shape[2]
    capacity = max(2, 2 * pair_dev // regions)
    partner = pair_orbitals[:, 1].reshape(regions, pair_dev)
    source = partner // occ_dev
    same_source = source[:, :, None] == source[:, None, :]
    positions = jnp.arange(pair_dev, dtype=jnp.int32)
    earlier = positions[None, :] < positions[:, None]
    slot_rank = jnp.sum(same_source & earlier[None], axis=2)
    first_orb = lax.dynamic_slice_in_dim(pair_orbitals[:, 0], region_index * pair_dev, pair_dev)
    my_partner = lax.dynamic_slice_in_dim(pair_orbitals[:, 1], region_index * pair_dev, pair_dev)
    my_rank = jnp.take(slot_rank, region_index, axis=0)
    slot_of_pair = my_partner // occ_dev * capacity + my_rank
    slot_ids = jnp.arange(regions * capacity, dtype=jnp.int32)
    match_out = slot_of_pair[None, :] == slot_ids[:, None]
    slot_pair = jnp.sum(jnp.where(match_out, positions[None, :], 0), axis=1)
    slot_used = jnp.any(match_out, axis=1)
    match_in = (source[:, None, :] == region_index) & (
        slot_rank[:, None, :] == jnp.arange(capacity, dtype=jnp.int32)[None, :, None]
    )
    local_orb = jnp.sum(
        jnp.where(match_in, partner[:, None, :] - region_index * occ_dev, 0), axis=2
    ).reshape(-1)
    local_used = jnp.any(match_in, axis=2).reshape(-1)
    first_maps = pno_maps[:, 0]
    second_maps = pno_maps[:, 1]
    first_rows = jnp.take(three_index, first_orb - region_index * occ_dev, axis=0)
    left_rows = jnp.einsum(
        "pkv,pva->pka", first_rows, first_maps, preferred_element_type=jnp.float32
    ).astype(jnp.bfloat16)
    outgoing = jnp.take(three_index, local_orb, axis=0).reshape(
        regions, capacity, aux_rows, virtuals
    )
    incoming = lax.all_to_all(outgoing, "region", split_axis=0, concat_axis=0, tiled=True)
    second_rows = jnp.take(
        incoming.reshape(regions * capacity, aux_rows, virtuals), slot_of_pair, axis=0
    )
    right_rows = jnp.einsum(
        "pkv,pva->pka", second_rows, second_maps, preferred_element_type=jnp.float32
    ).astype(jnp.bfloat16)
    partial_exchange = jnp.einsum(
        "pka,pkb->pab",
        left_rows,
        lax.all_gather(right_rows, "pno", axis=2, tiled=True),
        preferred_element_type=jnp.float32,
    )
    exchange = lax.psum(partial_exchange, "aux")
    extended = with_halo(amplitudes, (("region", 0),), pair_dev)
    near_index = neighbours - (region_index - 1) * pair_dev
    coupling = jnp.zeros((pair_dev, columns, width), jnp.float32)
    for neighbour in range(neighbours.shape[1]):
        taken = jnp.take(extended, near_index[:, neighbour], axis=0)
        coupling = coupling + couplings[:, neighbour][:, None, None] * taken.astype(jnp.float32)
    own_energies = lax.dynamic_slice_in_dim(pno_energies, pno_index * columns, columns, 1)
    occupied = jnp.take(occ_energies, first_orb) + jnp.take(occ_energies, my_partner)
    denominator = own_energies[:, :, None] + pno_energies[:, None, :] - occupied[:, None, None]
    row_ids = pno_index * columns + jnp.arange(columns, dtype=jnp.int32)
    col_ids = jnp.arange(width, dtype=jnp.int32)
    in_domain = (row_ids[None, :, None] < pno_counts[:, None, None]) & (
        col_ids[None, None, :] < pno_counts[:, None, None]
    )
    update = jnp.where(in_domain, (coupling - exchange) / denominator, jnp.float32(0.0))
    weight = (jnp.sum(update * update, axis=2) / width).astype(jnp.bfloat16)
    first_vec = jnp.einsum("pva,pa->pv", first_maps, weight, preferred_element_type=jnp.float32)
    second_vec = jnp.einsum("pva,pa->pv", second_maps, weight, preferred_element_type=jnp.float32)
    orbital_ids = jnp.arange(occ_dev, dtype=jnp.int32)
    first_onehot = ((first_orb - region_index * occ_dev)[None, :] == orbital_ids[:, None]).astype(
        jnp.float32
    )
    density = jnp.dot(first_onehot, first_vec, precision=lax.Precision.HIGHEST)
    send_vecs = jnp.where(
        slot_used[:, None], jnp.take(second_vec, slot_pair, axis=0), jnp.float32(0.0)
    )
    received = lax.all_to_all(
        send_vecs.reshape(regions, capacity, virtuals).astype(jnp.bfloat16),
        "region",
        split_axis=0,
        concat_axis=0,
        tiled=True,
    ).astype(jnp.float32)
    second_onehot = ((local_orb[None, :] == orbital_ids[:, None]) & local_used[None, :]).astype(
        jnp.float32
    )
    density = density + jnp.dot(
        second_onehot,
        received.reshape(regions * capacity, virtuals),
        precision=lax.Precision.HIGHEST,
    )
    density = lax.psum(density, "pno")
    return (update.astype(jnp.bfloat16), density)


def solution(mesh):
    in_specs = (
        P(("parts", "region"), "aux", None),
        P(("parts", "region"), None, None, "pno"),
        P(("parts", "region"), "pno", None),
        P("parts", None),
        P(("parts", "region"), None),
        P(("parts", "region"), None),
        P(("parts", "region"), None),
        P("parts"),
        P(("parts", "region")),
    )
    out_specs = (P(("parts", "region"), "pno", None), P(("parts", "region"), None))
    return jax.shard_map(body, mesh=mesh, in_specs=in_specs, out_specs=out_specs, check_vma=False)
```

profile of v0, /device:TPU:0, one launch (start us, length us, event | category | flops | bytes accessed | tf_op | source)
XLA Modules:
  0.0 747.6 jit_solution(16688297963209424371)
XLA Ops:
  7.2 0.0 copy-start
  7.2 0.9 and_reduce_fusion
  8.1 0.8 divide_reduce_fusion
  8.8 0.1 div.45
  8.9 0.1 and.118
  9.0 0.1 sub.73
  9.1 0.2 convert_reduce_fusion
  9.3 0.2 select_reduce_fusion
  9.5 0.1 reshape.286
  9.6 0.1 bitcast_add_fusion
  9.7 0.1 select_reduce_fusion.1
  9.8 0.0 copy-done
  9.8 9.8 %gather_fusion.1 = bf16[32,1536,256]{2,1,0:T(8,128)(2,1)} fusion(bf16[3,1536,256]{2,1,0:T(8,128)(2,1)S(1)} %copy-done, s32[1024]{0:T(1024)S(1)} %pad_clamp_fusion.4), kind=kCustom, calls=%fused_computation.7 | custom fusion | bytes 50331776 | tf_op jit(solution)/shard_map/jit(_take)/gather | solution.py:66
  19.6 21.1 %broadcast_select_fusion = bf16[4,8,1536,256]{3,2,1,0:T(8,128)(2,1)} fusion(bf16[4,8,1536,256]{3,2,1,0:T(8,128)(2,1)} %bitcast.90, pred[4,8]{1,0:T(4,128)(4,1)S(1)} %compare_and_fusion.5), kind=kLoop, calls=%fused_computation.10 | loop fusion | flops 12582912 | bytes 50331680 | tf_op jit(solution)/shard_map/jit(_take)/select_n | solution.py:66
  40.7 8.4 %all-to-all-start = ((bf16[4,8,1536,256]{3,2,1,0:T(8,128)(2,1)}), bf16[4,8,1536,256]{3,2,1,0:T(8,128)(2,1)}, u32[]{:S(2)}, u32[]{:S(2)}) async-start(bf16[4,8,1536,256]{3,2,1,0:T(8,128)(2,1)} %broadcast_select_fusion), calls=%async_computation | async-start | bytes 50331648 | tf_op jit(solution)/shard_map/all_to_all | solution.py:69
  49.2 0.0 all-gather.2.cloned.1.call-start
  49.2 0.1 and_bitcast_fusion
  49.3 544.2 %all-to-all-done = bf16[4,8,1536,256]{3,2,1,0:T(8,128)(2,1)} async-done(((bf16[4,8,1536,256]{3,2,1,0:T(8,128)(2,1)}), bf16[4,8,1536,256]{3,2,1,0:T(8,128)(2,1)}, u32[]{:S(2)}, u32[]{:S(2)}) %all-to-all-start) | async-done | bytes 25165856 | tf_op jit(solution)/shard_map/all_to_all | solution.py:69
  593.5 14.7 %gather_fusion.2 = bf16[16,1536,256]{2,1,0:T(8,128)(2,1)} fusion(bf16[32,1536,256]{2,1,0:T(8,128)(2,1)} %bitcast.15, s32[1024]{0:T(1024)S(1)} %pad_clamp_fusion.3), kind=kCustom, calls=%fused_computation.8 | custom fusion | bytes 25165888 | tf_op jit(solution)/shard_map/jit(_take)/gather | solution.py:70
  608.2 10.9 %fusion.10 = bf16[16,1536,128]{2,1,0:T(8,128)(2,1)} fusion(bf16[16,1536,256]{2,1,0:T(8,128)(2,1)} %gather_fusion.2, pred[16]{0:T(512)(128)(4,1)S(1)} %get-tuple-element.29, bf16[16,2,256,128]{3,2,1,0:T(8,128)(2,1)} %param.14), kind=kOutput, calls=%fused_computation.21 | convolution fusion | flops 1620049920 | bytes 19922960 | tf_op jit(solution)/shard_map/pkv,pva->pka/dot_general | solution.py:73
  619.1 0.0 all-gather.2.cloned.1.call-update
  619.1 0.0 all-reduce.2.cloned.1.call-start
  619.2 1.1 copy-done.3
  620.3 2.3 collective-permute-start
  622.6 1.5 collective-permute-start.1
  624.1 0.1 reduce_sum.44
  624.1 0.1 and_bitcast_fusion.1
  624.2 0.0 copy-start.5
  624.2 8.8 %gather_fusion = bf16[16,1536,256]{2,1,0:T(8,128)(2,1)} fusion(bf16[3,1536,256]{2,1,0:T(8,128)(2,1)S(1)} %copy-done, s32[1024]{0:T(1024)S(1)} %pad_clamp_fusion.5), kind=kCustom, calls=%fused_computation.6 | custom fusion | bytes 25165888 | tf_op jit(solution)/shard_map/jit(_take)/gather | solution.py:62
  633.0 0.1 bitcast_subtract_fusion
  633.1 0.0 copy-done.5
  633.2 10.2 %all-gather.2.cloned.1.call-done = bf16[16,1536,256]{2,1,0:T(8,128)(2,1)} async-done(((bf16[16,1536,128]{2,1,0:T(8,128)(2,1)}), bf16[16,1536,256]{2,1,0:T(8,128)(2,1)}) %all-gather.2.cloned.1.call-update) | async-done | bytes 12582928 | tf_op jit(solution)/shard_map/all_gather | solution.py:79
  643.3 12.7 %fusion.6 = f32[16,128,256]{2,1,0:T(8,128)} fusion(bf16[16,1536,256]{2,1,0:T(8,128)(2,1)} %all-gather.2.cloned.1.call-done, bf16[16,1536,256]{2,1,0:T(8,128)(2,1)} %gather_fusion, pred[16]{0:T(512)(128)(4,1)S(1)} %get-tuple-element.27, bf16[16,2,256,128]{3,2,1,0:T(8,128)(2,1)} %param.14), kind=kOutput, calls=%fused_computation.17 | convolution fusion | flops 3230662656 | bytes 28311568 | tf_op jit(solution)/shard_map/pka,pkb->pab/dot_general | solution.py:76
  656.0 0.0 all-reduce.2.cloned.1.call-update
  656.0 0.0 copy-done.4
  656.1 0.1 fusion.36
  656.2 0.1 fusion.37
  656.3 0.1 reshape.288
  656.4 0.7 gather_fusion.8
  657.1 0.7 gather_fusion.9
  657.7 0.1 broadcast_in_dim.132
  657.8 0.1 and.125
  657.9 0.1 broadcast_compare_fusion
  658.0 0.1 iota_compare_fusion.1
  658.1 0.0 collective-permute-done
  658.1 2.3 constant_dynamic-update-slice_fusion.2
  660.4 1.1 constant_dynamic-update-slice_fusion.1
  661.5 0.0 collective-permute-done.1
  661.5 2.4 constant_dynamic-update-slice_fusion
  663.9 2.5 gather_fusion.4
  666.4 3.5 gather_fusion.5
  669.9 3.5 gather_fusion.6
  673.4 3.5 gather_fusion.7
  676.9 43.4 %all-reduce.2.cloned.1.call-done = f32[16,128,256]{2,1,0:T(8,128)} async-done(((f32[16,128,256]{2,1,0:T(8,128)}), f32[16,128,256]{2,1,0:T(8,128)}) %all-reduce.2.cloned.1.call-update) | async-done | bytes 2097168 | tf_op jit(solution)/shard_map/psum | solution.py:82
  720.3 5.0 multiply_reduce_fusion
  725.3 0.4 fusion.17
  725.7 0.4 fusion.20
  726.1 0.6 gather_fusion.3
  726.7 0.7 fusion.30
  727.4 4.6 all-to-all-start.1
  732.0 0.1 fusion.32
  732.1 5.5 all-to-all-done.1
  737.6 0.1 convolution_add_fusion
  737.7 3.0 psum.15
  (30 shorter events, 0.1 us)
Async XLA Ops:
  7.2 2.6 copy-start
  40.7 552.7 %all-to-all-start = ((bf16[4,8,1536,256]{3,2,1,0:T(8,128)(2,1)}), bf16[4,8,1536,256]{3,2,1,0:T(8,128)(2,1)}, u32[]{:S(2)}, u32[]{:S(2)}) async-start(bf16[4,8,1536,256]{3,2,1,0:T(8,128)(2,1)} %broadcast_select_fusion), calls=%async_computation | async-start | bytes 50331648 | tf_op jit(solution)/shard_map/all_to_all | solution.py:69
  49.2 594.2 %all-gather.2.cloned.1.call-start = ((), (), s32[]{:S(2)}) async-start(), calls=%async_computation.2 | async-start | bytes 18874368 | tf_op jit(solution)/shard_map/all_gather | solution.py:79
  619.1 1.2 copy-start.3
  619.1 101.2 %all-reduce.2.cloned.1.call-start = ((), (), s32[]{:S(2)}) async-start(), calls=%async_computation.3 | async-start | bytes 4194304 | tf_op jit(solution)/shard_map/psum | solution.py:82
  620.3 37.8 %collective-permute-start = (bf16[16,128,256]{2,1,0:T(8,128)(2,1)S(1)}, bf16[16,128,256]{2,1,0:T(8,128)(2,1)}, u32[]{:S(2)}, u32[]{:S(2)}) collective-permute-start(bf16[16,128,256]{2,1,0:T(8,128)(2,1)S(1)} %copy-done.3), channel_id=1, source_target_pairs={{0,4},{4,8},{8,12},{1,5},{5,9},{9,13},{2,6},{6,10},{10,14},{3,7},{... | collective-permute-start | bytes 3145736 | tf_op jit(solution)/shard_map/ppermute | solution.py:12
  622.6 38.9 %collective-permute-start.1 = (bf16[16,128,256]{2,1,0:T(8,128)(2,1)S(1)}, bf16[16,128,256]{2,1,0:T(8,128)(2,1)}, u32[]{:S(2)}, u32[]{:S(2)}) collective-permute-start(bf16[16,128,256]{2,1,0:T(8,128)(2,1)S(1)} %copy-done.3), channel_id=1, source_target_pairs={{4,0},{8,4},{12,8},{5,1},{9,5},{13,9},{6,2},{10,6},{14,10},{7,3},{... | collective-permute-start | bytes 3145736 | tf_op jit(solution)/shard_map/ppermute | solution.py:15
  624.2 8.9 %copy-start.5 = (s32[16,4]{0,1:T(4,128)S(1)}, s32[16,4]{0,1:T(4,128)}, u32[]{:S(2)}) copy-start(s32[16,4]{0,1:T(4,128)} %param.17) | copy-start | bytes 772
  643.3 12.7 %copy-start.4 = (f32[16,256]{1,0:T(8,128)S(1)}, f32[16,256]{1,0:T(8,128)}, u32[]{:S(2)}) copy-start(f32[16,256]{1,0:T(8,128)} %param.19) | copy-start | bytes 49156
  643.3 13.1 %copy-start.1 = (f32[12]{0:T(128)S(1)}, f32[12]{0:T(128)}, u32[]{:S(2)}) copy-start(f32[12]{0:T(128)} %param.20) | copy-start | bytes 148
  656.0 1.9 copy-start.7
  656.0 2.0 copy-start.6
  720.3 5.0 copy-start.2
  727.4 10.2 %all-to-all-start.1 = ((bf16[4,8,256]{2,1,0:T(8,128)(2,1)}), bf16[4,8,256]{2,1,0:T(8,128)(2,1)S(1)}, u32[]{:S(2)}, u32[]{:S(2)}) async-start(bf16[4,8,256]{2,1,0:T(8,128)(2,1)} %fusion.30), calls=%async_computation.1 | async-start | bytes 32768 | tf_op jit(solution)/shard_map/all_to_all | solution.py:109
Sparse Core Ops, SparseCore 0:
  619.2 24.0 all-gather.1
  656.2 64.1 all-reduce.1
where the time goes:
time: 748 us
  waiting for transfers between devices  603 us (81%)
  local copies, waits for them, and re-layouts  55.9 us (7%)
  other arithmetic  29.7 us (4%)
  matrix products  24.6 us (3%)
  starting transfers between devices  16.8 us (2%)
  between operations  14.3 us (2%)
    all_to_all x1, waiting for transfers between devices, body(): lax.all_to_all(outgoing, 'region', split_axis=0, concat_axis=0, tiled=True)  544 us
    psum x1, waiting for transfers between devices, body(): exchange = lax.psum(partial_exchange, 'aux')  43.4 us
    select_n x2, other arithmetic, body(): jnp.take(three_index, local_orb, axis=0)  21.2 us
  transfers between devices with their start and end apart: 6, of which 4 were waited for; matrix products, arithmetic and copies ran while one was open for 6% of the time, Pallas kernels for 0%

commit v1 on v0

--- a/solution.py
+++ b/solution.py
@@ -59,27 +59,24 @@
     local_used = jnp.any(match_in, axis=2).reshape(-1)
     first_maps = pno_maps[:, 0]
     second_maps = pno_maps[:, 1]
-    first_rows = jnp.take(three_index, first_orb - region_index * occ_dev, axis=0)
-    left_rows = jnp.einsum(
-        "pkv,pva->pka", first_rows, first_maps, preferred_element_type=jnp.float32
-    ).astype(jnp.bfloat16)
-    outgoing = jnp.take(three_index, local_orb, axis=0).reshape(
-        regions, capacity, aux_rows, virtuals
+    regions_pno = lax.axis_size("pno")
+    part_rows = aux_rows // regions_pno
+    own_rows = lax.dynamic_slice_in_dim(three_index, pno_index * part_rows, part_rows, axis=1)
+    all_rows = lax.all_gather(own_rows, "region", axis=0, tiled=True)
+    gram = jnp.einsum("ikv,jkw->ijvw", own_rows, all_rows, preferred_element_type=jnp.float32)
+    gram = gram.astype(jnp.bfloat16).reshape(-1, virtuals, virtuals)
+    pair_gram = jnp.take(
+        gram, (first_orb - region_index * occ_dev) * (regions * occ_dev) + my_partner, axis=0
     )
-    incoming = lax.all_to_all(outgoing, "region", split_axis=0, concat_axis=0, tiled=True)
-    second_rows = jnp.take(
-        incoming.reshape(regions * capacity, aux_rows, virtuals), slot_of_pair, axis=0
-    )
-    right_rows = jnp.einsum(
-        "pkv,pva->pka", second_rows, second_maps, preferred_element_type=jnp.float32
+    full_maps = lax.all_gather(pno_maps, "pno", axis=3, tiled=True)
+    half_way = jnp.einsum(
+        "pva,pvw->paw", full_maps[:, 0], pair_gram, preferred_element_type=jnp.float32
     ).astype(jnp.bfloat16)
     partial_exchange = jnp.einsum(
-        "pka,pkb->pab",
-        left_rows,
-        lax.all_gather(right_rows, "pno", axis=2, tiled=True),
-        preferred_element_type=jnp.float32,
+        "paw,pwb->pab", half_way, full_maps[:, 1], preferred_element_type=jnp.float32
     )
-    exchange = lax.psum(partial_exchange, "aux")
+    partial_exchange = lax.psum_scatter(partial_exchange, "pno", scatter_dimension=1, tiled=True)
+    exchange = lax.psum(partial_exchange.astype(jnp.bfloat16), "aux").astype(jnp.float32)
     extended = with_halo(amplitudes, (("region", 0),), pair_dev)
     near_index = neighbours - (region_index - 1) * pair_dev
     coupling = jnp.zeros((pair_dev, columns, width), jnp.float32)

time: 748 us -> 210 us (0.28)
  waiting for transfers between devices: 603 us -> 118 us
  other arithmetic: 29.7 us -> 10.4 us
  local copies, waits for them, and re-layouts: 55.9 us -> 40.4 us
  matrix products: 24.6 us -> 15 us
  starting transfers between devices: 16.8 us -> 8.32 us
    all_to_all x1 -> x0, waiting for transfers between devices: 544 us -> none  [body(): lax.all_to_all(outgoing, 'region', split_axis=0, concat_axis=0, tiled=True)]
    all_gather x1 -> x2, waiting for transfers between devices: 10.2 us -> 87.3 us  [the longest x1 87.3 us: body(): all_rows = lax.all_gather(own_rows, 'region', axis=0, tiled=True)]
    psum x1, waiting for transfers between devices: 43.4 us -> 8.96 us  [body(): lax.psum(partial_exchange.astype(jnp.bfloat16), 'aux').astype(jnp.float32)]
    gather x3 -> x1, local copies, waits for them, and re-layouts: 33.3 us -> 4.4 us  [body(): jnp.take(gram, (first_orb - region_index * occ_dev) * (regions * occ_dev)...]
    select_n x2 -> x1, other arithmetic: 21.2 us -> 0.01 us  [body(): jnp.take(second_vec, slot_pair, axis=0)]
    ppermute x1, waiting for transfers between devices: 0.01 us -> 11.7 us  [with_halo(): lax.ppermute(lax.slice_in_dim(block, block.shape[dim] - width, None, axis...]
    dot_general x2, matrix products: 23.6 us -> 14 us  [the longest x1 7.84 us: body(): jnp.einsum('ikv,jkw->ijvw', own_rows, all_rows, preferred_element_type=jn...]
    all_to_all x1 -> x0, starting transfers between devices: 8.42 us -> none  [body(): lax.all_to_all(outgoing, 'region', split_axis=0, concat_axis=0, tiled=True)]
  transfers between devices with their start and end apart: 6 -> 7, of which waited for: 4 -> 6; matrix products, arithmetic and copies ran while one was open for 6% -> 23% of each run, Pallas kernels for 0% -> 0%
where the time goes in v1:
time: 210 us; the launch traced here: 209 us
  waiting for transfers between devices  118 us (56%)
  local copies, waits for them, and re-layouts  40.4 us (19%)
  matrix products  15 us (7%)
  between operations  14 us (7%)
  other arithmetic  10.4 us (5%)
  starting transfers between devices  8.32 us (4%)
  blocking collectives  3.03 us (1%)
    all_gather x1, waiting for transfers between devices, body(): all_rows = lax.all_gather(own_rows, 'region', axis=0, tiled=True)  87.3 us
    gather x4, local copies, waits for them, and re-layouts, body(): taken = jnp.take(extended, near_index[:, neighbour], axis=0)  13.2 us
    ppermute x1, waiting for transfers between devices, with_halo(): lax.ppermute(lax.slice_in_dim(block, block.shape[dim] - width, None, axis...  11.7 us
    unnamed x29, local copies, waits for them, and re-layouts  9.87 us
    psum x1, waiting for transfers between devices, body(): lax.psum(partial_exchange.astype(jnp.bfloat16), 'aux').astype(jnp.float32)  8.96 us
    dot_general x1, matrix products, body(): jnp.einsum('ikv,jkw->ijvw', own_rows, all_rows, preferred_element_type=jn...  7.84 us
    convert_element_type x1, local copies, waits for them, and re-layouts, body(): gram = gram.astype(jnp.bfloat16).reshape(-1, virtuals, virtuals)  6.89 us
    dot_general x1, matrix products, body(): jnp.einsum('paw,pwb->pab', half_way, full_maps[:, 1], preferred_element_t...  6.2 us
  transfers between devices with their start and end apart: 7, of which 6 were waited for; matrix products, arithmetic and copies ran while one was open for 23% of the time, Pallas kernels for 0%

profile of v1, /device:TPU:0, one launch (start us, length us, event | category | flops | bytes accessed | tf_op | source)
XLA Modules:
  0.0 209.4 jit_solution(18365409572481940197)
XLA Ops:
  7.2 0.0 copy-start
  7.2 0.0 all-gather.3.cloned.1.call-start
  7.2 1.6 copy-done
  8.8 1.1 constant_dynamic-slice_fusion.2
  10.0 0.0 all-gather.3.cloned.1.call-update
  10.0 0.0 all-gather.5.cloned.1.call-start
  10.0 3.1 %copy.23 = bf16[16,2,256,128]{3,2,0,1:T(8,128)(2,1)} copy(bf16[16,2,256,128]{3,2,1,0:T(8,128)(2,1)} %param.14) | data formatting | bytes 4194304 | tf_op args[1]
  13.2 0.0 all-gather.5.cloned.1.call-update
  13.2 0.0 reduce-scatter.2.cloned.1.call-start
  13.3 0.6 copy-done.10
  13.9 0.5 subtract_reduce_fusion
  14.4 0.6 and_bitcast_fusion
  15.0 87.3 %all-gather.3.cloned.1.call-done = bf16[12,768,256]{2,1,0:T(8,128)(2,1)} async-done(((bf16[3,768,256]{2,1,0:T(8,128)(2,1)}), bf16[12,768,256]{2,1,0:T(8,128)(2,1)}) %all-gather.3.cloned.1.call-update) | async-done | bytes 4718608 | tf_op jit(solution)/shard_map/all_gather | solution.py:65
  102.3 7.8 %convert_bitcast_fusion = bf16[3,12,256,256]{2,3,0,1:T(8,128)(2,1)} fusion(bf16[12,768,256]{2,1,0:T(8,128)(2,1)} %all-gather.3.cloned.1.call-done, bf16[3,768,256]{2,1,0:T(8,128)(2,1)S(1)} %copy-done.3), kind=kOutput, calls=%fused_computation.10 | convolution fusion | flops 3626237952 | bytes 10616832 | tf_op jit(solution)/shard_map/ikv,jkw->ijvw/dot_general | solution.py:66
  110.1 6.9 %copy.22 = bf16[3,12,256,256]{3,2,1,0:T(8,128)(2,1)} copy(bf16[3,12,256,256]{2,3,0,1:T(8,128)(2,1)} %convert_bitcast_fusion) | data formatting | bytes 9437184 | tf_op jit(solution)/shard_map/convert_element_type | solution.py:67
  117.0 4.4 %gather_fusion = bf16[16,256,256]{2,1,0:T(8,128)(2,1)} fusion(bf16[36,256,256]{2,1,0:T(8,128)(2,1)} %bitcast.93, s32[1024]{0:T(1024)S(1)} %pad_clamp_fusion.3), kind=kCustom, calls=%fused_computation.6 | custom fusion | bytes 4194368 | tf_op jit(solution)/shard_map/jit(_take)/gather | solution.py:68
  121.4 6.2 %fusion.4 = f32[16,256,256]{2,1,0:T(8,128)} fusion(bf16[16,2,256,256]{3,2,0,1:T(8,128)(2,1)} %all-gather.5.cloned.1.call-done, bf16[16,256,256]{2,1,0:T(8,128)(2,1)} %gather_fusion, pred[16]{0:T(512)(128)(4,1)S(1)} %copy-done.12), kind=kOutput, calls=%fused_computation.12 | convolution fusion | flops 1075838976 | bytes 10485776 | tf_op jit(solution)/shard_map/paw,pwb->pab/dot_general | solution.py:75
  127.6 0.0 copy-start.1
  127.6 0.0 copy-start.9
  127.7 0.0 reduce-scatter.2.cloned.1.call-update
  127.7 0.0 all-reduce.2.cloned.1.call-start
  127.7 1.1 copy-done.4
  128.8 2.3 %collective-permute-start = (bf16[16,128,256]{2,1,0:T(8,128)(2,1)S(1)}, bf16[16,128,256]{2,1,0:T(8,128)(2,1)}, u32[]{:S(2)}, u32[]{:S(2)}) collective-permute-start(bf16[16,128,256]{2,1,0:T(8,128)(2,1)S(1)} %copy-done.4), channel_id=1, source_target_pairs={{0,4},{4,8},{8,12},{1,5},{5,9},{9,13},{2,6},{6,10},{10,14},{3,7},{... | collective-permute-start | bytes 3145736 | tf_op jit(solution)/shard_map/ppermute | solution.py:12
  131.1 1.3 collective-permute-start.1
  132.4 0.1 div.43
  132.5 0.1 and.98
  132.6 0.2 convert_reduce_fusion
  132.8 0.1 fusion.38
  132.9 0.1 select_reduce_fusion.1
  133.0 0.1 reduce_sum.44
  133.1 0.1 sub.75
  133.3 0.1 fusion.27
  133.5 0.2 select_reduce_fusion
  133.6 0.1 fusion.28
  133.8 0.7 gather_fusion.6
  134.4 0.7 gather_fusion.7
  135.1 0.1 broadcast_in_dim.111
  135.2 0.1 eq.89
  135.3 0.1 and.103
  135.3 0.1 broadcast_compare_fusion
  135.4 2.9 %reduce-scatter.2.cloned.1.call-done = f32[16,128,256]{2,1,0:T(8,128)} async-done(((f32[16,256,256]{2,1,0:T(8,128)}), f32[16,128,256]{2,1,0:T(8,128)}) %reduce-scatter.2.cloned.1.call-update) | async-done | bytes 2097168 | tf_op jit(solution)/shard_map/reduce_scatter | solution.py:78
  138.4 2.7 %convert_element_type.50 = bf16[16,128,256]{2,1,0:T(8,128)(2,1)} convert(f32[16,128,256]{2,1,0:T(8,128)} %reduce-scatter.2.cloned.1.call-done) | non-fusion elementwise | flops 524288 | bytes 3145728 | tf_op jit(solution)/shard_map/convert_element_type | solution.py:79
  141.1 0.0 all-reduce.2.cloned.1.call-update
  141.1 0.1 iota_compare_fusion.1
  141.2 11.7 %collective-permute-done = bf16[16,128,256]{2,1,0:T(8,128)(2,1)} collective-permute-done((bf16[16,128,256]{2,1,0:T(8,128)(2,1)S(1)}, bf16[16,128,256]{2,1,0:T(8,128)(2,1)}, u32[]{:S(2)}, u32[]{:S(2)}) %collective-permute-start) | collective-permute-done | bytes 1048608 | tf_op jit(solution)/shard_map/ppermute | solution.py:12
  152.9 2.3 %constant_dynamic-update-slice_fusion.2 = bf16[48,128,256]{2,1,0:T(8,128)(2,1)} fusion(bf16[16,128,256]{2,1,0:T(8,128)(2,1)} %collective-permute-done), kind=kLoop, calls=%fused_computation.52 | loop fusion | bytes 2097152
  155.2 1.1 constant_dynamic-update-slice_fusion.1
  156.3 1.8 collective-permute-done.1
  158.1 2.3 %constant_dynamic-update-slice_fusion = bf16[48,128,256]{2,1,0:T(8,128)(2,1)} fusion(bf16[48,128,256]{2,1,0:T(8,128)(2,1)} %constant_dynamic-update-slice_fusion.1, bf16[16,128,256]{2,1,0:T(8,128)(2,1)} %collective-permute-done.1), kind=kLoop, calls=%fused_computation.50 | loop fusion | bytes 2097152 | tf_op jit(solution)/shard_map/concatenate | solution.py:16
  160.4 2.5 %gather_fusion.4 = bf16[16,128,256]{2,1,0:T(8,128)(2,1)S(1)} fusion(bf16[48,128,256]{2,1,0:T(8,128)(2,1)} %constant_dynamic-update-slice_fusion, s32[1024]{0:T(1024)S(1)} %get-tuple-element.50), kind=kCustom, calls=%fused_computation.3.clone | custom fusion | bytes 2097216 | tf_op jit(solution)/shard_map/jit(_take)/gather | solution.py:84
  162.9 3.5 %gather_fusion.5 = bf16[16,128,256]{2,1,0:T(8,128)(2,1)} fusion(bf16[48,128,256]{2,1,0:T(8,128)(2,1)} %constant_dynamic-update-slice_fusion, s32[1024]{0:T(1024)S(1)} %get-tuple-element.49), kind=kCustom, calls=%fused_computation.4.clone | custom fusion | bytes 2097216 | tf_op jit(solution)/shard_map/jit(_take)/gather | solution.py:84
  166.4 3.6 %gather_fusion.2 = bf16[16,128,256]{2,1,0:T(8,128)(2,1)} fusion(bf16[48,128,256]{2,1,0:T(8,128)(2,1)} %constant_dynamic-update-slice_fusion, s32[1024]{0:T(1024)S(1)} %get-tuple-element.52), kind=kCustom, calls=%fused_computation.clone | custom fusion | bytes 2097216 | tf_op jit(solution)/shard_map/jit(_take)/gather | solution.py:84
  170.0 3.6 %gather_fusion.3 = bf16[16,128,256]{2,1,0:T(8,128)(2,1)} fusion(bf16[48,128,256]{2,1,0:T(8,128)(2,1)} %constant_dynamic-update-slice_fusion, s32[1024]{0:T(1024)S(1)} %get-tuple-element.51), kind=kCustom, calls=%fused_computation.2.clone | custom fusion | bytes 2097216 | tf_op jit(solution)/shard_map/jit(_take)/gather | solution.py:84
  173.6 9.0 %all-reduce.2.cloned.1.call-done = bf16[16,128,256]{2,1,0:T(8,128)(2,1)} async-done(((bf16[16,128,256]{2,1,0:T(8,128)(2,1)}), bf16[16,128,256]{2,1,0:T(8,128)(2,1)}) %all-reduce.2.cloned.1.call-update) | async-done | bytes 1048592 | tf_op jit(solution)/shard_map/psum | solution.py:79
  182.5 4.8 %multiply_reduce_fusion = (f32[16,128]{1,0:T(8,128)S(1)}, bf16[16,128,256]{2,1,0:T(8,128)(2,1)}) fusion(f32[16]{0:T(128)S(1)} %fusion.39, f32[16,256]{1,0:T(8,128)S(1)} %copy-done.5, f32[16,128]{1,0:T(8,128)S(1)} %constant_dynamic-slice_fusion.1, bf16[16,128,256]{2,1,0:T(8,128)(2,1)} %all-reduce.2.cloned.1.call-done, bf16[16,128,256]{2,1,0:T(8,128)(2,1)} %gather_fusion.5, ...), kind=kLoop, calls=%fused_computation.15 | loop fusion | flops 13105152 | bytes 6330752 | tf_op jit(solution)/shard_map/reduce_sum | solution.py:95
  187.4 0.4 fusion.12
  187.8 0.4 fusion.14
  188.2 0.6 gather_fusion.1
  188.8 0.7 fusion.21
  189.5 4.6 %all-to-all-start = ((bf16[4,8,256]{2,1,0:T(8,128)(2,1)}), bf16[4,8,256]{2,1,0:T(8,128)(2,1)S(1)}, u32[]{:S(2)}, u32[]{:S(2)}) async-start(bf16[4,8,256]{2,1,0:T(8,128)(2,1)} %fusion.21), calls=%async_computation.1 | async-start | bytes 32768 | tf_op jit(solution)/shard_map/all_to_all | solution.py:106
  194.1 0.1 fusion.23
  194.2 5.5 %all-to-all-done = bf16[4,8,256]{2,1,0:T(8,128)(2,1)S(1)} async-done(((bf16[4,8,256]{2,1,0:T(8,128)(2,1)}), bf16[4,8,256]{2,1,0:T(8,128)(2,1)S(1)}, u32[]{:S(2)}, u32[]{:S(2)}) %all-to-all-start) | async-done | bytes 16416 | tf_op jit(solution)/shard_map/all_to_all | solution.py:106
  199.7 0.1 convolution_add_fusion
  199.8 3.0 %psum.15 = f32[3,256]{1,0:T(4,128)} all-reduce(f32[3,256]{1,0:T(4,128)S(1)} %convolution_add_fusion), channel_id=1, replica_groups=mesh['parts'=2,'region'=4,'aux'=2,'pno'=2] {'pno'}, use_global_device_ids=true, to_apply=%region_8.11 | all-reduce | flops 768 | bytes 6144 | tf_op jit(solution)/shard_map/psum | solution.py:121
  (40 shorter events, 0.2 us)
Async XLA Ops:
  7.2 1.7 copy-start
  7.2 95.1 %all-gather.3.cloned.1.call-start = ((), (), s32[]{:S(2)}) async-start(), calls=%async_computation.2 | async-start | bytes 5898240 | tf_op jit(solution)/shard_map/all_gather | solution.py:65
  10.0 111.4 %all-gather.5.cloned.1.call-start = ((), (), s32[]{:S(2)}) async-start(), calls=%async_computation.3 | async-start | bytes 6291456 | tf_op jit(solution)/shard_map/all_gather | solution.py:71
  13.2 0.7 copy-start.10
  13.2 89.1 %copy-start.3 = (bf16[3,768,256]{2,1,0:T(8,128)(2,1)S(1)}, bf16[3,768,256]{2,1,0:T(8,128)(2,1)}, u32[]{:S(2)}) copy-start(bf16[3,768,256]{2,1,0:T(8,128)(2,1)} %constant_dynamic-slice_fusion.2) | copy-start | bytes 3538948
  13.2 125.2 %reduce-scatter.2.cloned.1.call-start = ((), (), s32[]{:S(2)}) async-start(), calls=%async_computation.4 | async-start | bytes 6291456 | tf_op jit(solution)/shard_map/reduce_scatter | solution.py:78
  117.0 4.4 %copy-start.12 = (pred[16]{0:T(512)(128)(4,1)S(1)}, pred[16]{0:T(512)(128)(4,1)}, u32[]{:S(2)}) copy-start(pred[16]{0:T(512)(128)(4,1)} %get-tuple-element.29) | copy-start | bytes 52
  127.6 1.2 copy-start.4
  127.6 4.8 %copy-start.6 = (s32[64]{0:T(128)S(1)}, s32[64]{0:T(128)}, u32[]{:S(2)}) copy-start(s32[64]{0:T(128)} %get-tuple-element.16) | copy-start | bytes 772
  127.6 4.9 %copy-start.11 = (s32[64,2]{0,1:T(2,128)S(1)}, s32[64,2]{0,1:T(2,128)}, u32[]{:S(2)}) copy-start(s32[64,2]{0,1:T(2,128)} %param.16) | copy-start | bytes 1540
  127.6 5.6 %copy-start.7 = (s32[16,4]{0,1:T(4,128)S(1)}, s32[16,4]{0,1:T(4,128)}, u32[]{:S(2)}) copy-start(s32[16,4]{0,1:T(4,128)} %param.17) | copy-start | bytes 772
  127.6 5.7 %copy-start.5 = (f32[16,256]{1,0:T(8,128)S(1)}, f32[16,256]{1,0:T(8,128)}, u32[]{:S(2)}) copy-start(f32[16,256]{1,0:T(8,128)} %param.19) | copy-start | bytes 49156
  127.6 6.1 %copy-start.1 = (f32[12]{0:T(128)S(1)}, f32[12]{0:T(128)}, u32[]{:S(2)}) copy-start(f32[12]{0:T(128)} %param.20) | copy-start | bytes 148
  127.6 7.7 %copy-start.9 = (s32[16]{0:T(128)S(1)}, s32[16]{0:T(128)}, u32[]{:S(2)}) copy-start(s32[16]{0:T(128)} %param.21) | copy-start | bytes 196
  127.7 54.9 %all-reduce.2.cloned.1.call-start = ((), (), s32[]{:S(2)}) async-start(), calls=%async_computation.5 | async-start | bytes 2097152 | tf_op jit(solution)/shard_map/psum | solution.py:79
  128.8 24.1 %collective-permute-start = (bf16[16,128,256]{2,1,0:T(8,128)(2,1)S(1)}, bf16[16,128,256]{2,1,0:T(8,128)(2,1)}, u32[]{:S(2)}, u32[]{:S(2)}) collective-permute-start(bf16[16,128,256]{2,1,0:T(8,128)(2,1)S(1)} %copy-done.4), channel_id=1, source_target_pairs={{0,4},{4,8},{8,12},{1,5},{5,9},{9,13},{2,6},{6,10},{10,14},{3,7},{... | collective-permute-start | bytes 3145736 | tf_op jit(solution)/shard_map/ppermute | solution.py:12
  131.1 27.0 %collective-permute-start.1 = (bf16[16,128,256]{2,1,0:T(8,128)(2,1)S(1)}, bf16[16,128,256]{2,1,0:T(8,128)(2,1)}, u32[]{:S(2)}, u32[]{:S(2)}) collective-permute-start(bf16[16,128,256]{2,1,0:T(8,128)(2,1)S(1)} %copy-done.4), channel_id=1, source_target_pairs={{4,0},{8,4},{12,8},{5,1},{9,5},{13,9},{6,2},{10,6},{14,10},{7,3},{... | collective-permute-start | bytes 3145736 | tf_op jit(solution)/shard_map/ppermute | solution.py:15
  135.4 5.7 %copy-start.8 = (f32[16,4]{0,1:T(4,128)S(1)}, f32[16,4]{0,1:T(4,128)}, u32[]{:S(2)}) copy-start(f32[16,4]{0,1:T(4,128)} %param.18) | copy-start | bytes 772
  182.5 4.9 %copy-start.2 = (bf16[16,2,256,128]{3,2,1,0:T(8,128)(2,1)S(1)}, bf16[16,2,256,128]{3,2,1,0:T(8,128)(2,1)}, u32[]{:S(2)}) copy-start(bf16[16,2,256,128]{3,2,1,0:T(8,128)(2,1)} %param.14) | copy-start | bytes 6291460
  189.5 10.2 %all-to-all-start = ((bf16[4,8,256]{2,1,0:T(8,128)(2,1)}), bf16[4,8,256]{2,1,0:T(8,128)(2,1)S(1)}, u32[]{:S(2)}, u32[]{:S(2)}) async-start(bf16[4,8,256]{2,1,0:T(8,128)(2,1)} %fusion.21), calls=%async_computation.1 | async-start | bytes 32768 | tf_op jit(solution)/shard_map/all_to_all | solution.py:106
Sparse Core Ops, SparseCore 0:
  10.1 92.0 all-gather.2
  103.8 11.4 all-gather.4
  127.8 10.5 reduce-scatter.1
  141.2 41.2 all-reduce.1

commit v2 on v1

v2 whole, which is shorter than its diff:
```python
import functools

import jax
import jax.numpy as jnp
from jax import lax
from jax.experimental import pallas as pl
from jax.experimental.pallas import tpu as pltpu
from jax.sharding import PartitionSpec as P

MESH = pl.DeviceIdType.MESH
F32 = jnp.float32
BF16 = jnp.bfloat16
CHUNK = 4


def exchange_kernel(
    regions,
    peers,
    first_ref,
    partner_ref,
    rows_ref,
    maps_ref,
    out_ref,
    own_t,
    edge_t,
    far_rows,
    gram,
    edge_gram,
    second_maps,
    first_t,
    partials,
    link_send,
    link_recv,
    core_send,
    core_recv,
    edge_send,
    maps_send,
    maps_recv,
    peer_send,
    peer_recv,
):
    occ, aux_rows, virtuals = rows_ref.shape
    pairs = maps_ref.shape[0]
    columns = maps_ref.shape[3]
    z = lax.axis_index("region")
    core = lax.axis_index("pno")
    mine = lax.axis_index("aux")
    part = aux_rows // 2
    half = virtuals // 2
    steps = (regions - 1) * occ
    slots = 2 * occ
    row_part = pl.ds(pl.multiple_of(core * part, part), part)
    row_rest = pl.ds(pl.multiple_of((1 - core) * part, part), part)
    gram_part = pl.ds(pl.multiple_of(core * half, half), half)
    gram_rest = pl.ds(pl.multiple_of((1 - core) * half, half), half)
    own_columns = pl.ds(pl.multiple_of(core * columns, columns), columns)
    sibling = {"pno": 1 - core}

    barrier = pltpu.get_barrier_semaphore()
    pl.semaphore_signal(barrier, inc=1, device_id=sibling, device_id_type=MESH)
    for k in range(1, peers):
        pl.semaphore_signal(
            barrier, inc=1, device_id={"aux": lax.rem(mine + k, peers)}, device_id_type=MESH
        )

    @pl.when(z > 0)
    def _():
        pl.semaphore_signal(barrier, inc=1, device_id={"region": z - 1}, device_id_type=MESH)

    @pl.when(z < regions - 1)
    def _():
        pl.semaphore_signal(barrier, inc=1, device_id={"region": z + 1}, device_id_type=MESH)

    neighbours = jnp.where(z > 0, 1, 0) + jnp.where(z < regions - 1, 1, 0)
    pl.semaphore_wait(barrier, peers + neighbours)

    def remote(src, dst, send, recv, device):
        return pltpu.make_async_remote_copy(
            src_ref=src,
            dst_ref=dst,
            send_sem=send,
            recv_sem=recv,
            device_id=device,
            device_id_type=MESH,
        )

    ahead = (z + 1, z - 1)
    ahead_exists = (z < regions - 1, z > 0)
    ahead_is_end = (z == regions - 2, z == 1)
    ahead_goes_on = (z < regions - 2, z > 1)
    at_end = (z == regions - 1, z == 0)

    def source(d, e):
        region = z - 1 - e // occ if d == 0 else z + 1 + e // occ
        return region, (region >= 0) & (region < regions), region * occ + lax.rem(e, occ)

    def own_copy(d, o):
        return remote(
            rows_ref.at[o, row_part],
            far_rows.at[z * occ + o, row_part],
            link_send.at[d, o],
            link_recv.at[d, o],
            {"region": ahead[d]},
        )

    def onward_copy(d, e, orbital):
        return remote(
            far_rows.at[orbital, row_part],
            far_rows.at[orbital, row_part],
            link_send.at[d, e + occ],
            link_recv.at[d, e + occ],
            {"region": ahead[d]},
        )

    def rows_to_core(d, e, orbital, which):
        return remote(
            far_rows.at[orbital, which],
            far_rows.at[orbital, which],
            core_send.at[d, e],
            core_recv.at[d, e],
            sibling,
        )

    def gram_to_core(d, e, orbital, which):
        return remote(
            gram.at[orbital, :, which],
            gram.at[orbital, :, which],
            core_send.at[d, e],
            core_recv.at[d, e],
            sibling,
        )

    def edge_copy(d, e, orbital):
        slot = lax.rem(e, slots)
        return remote(
            edge_gram.at[slot, :, gram_part],
            gram.at[orbital, :, gram_part],
            edge_send.at[slot],
            link_recv.at[d, e + occ],
            {"region": ahead[d]},
        )

    def maps_copy():
        return remote(
            maps_ref.at[:, 1],
            second_maps.at[:, :, own_columns],
            maps_send,
            maps_recv,
            sibling,
        )

    for d in range(2):

        @pl.when(ahead_exists[d])
        def _(d=d):
            for o in range(occ):
                own_copy(d, o).start()

    maps_copy().start()
    for o in range(occ):
        own_t[o] = rows_ref[o].T

    def own_gram(o, carry):
        for i in range(occ):
            gram[z * occ + o, i] = jnp.dot(
                own_t[i], rows_ref[o], preferred_element_type=F32
            ).astype(BF16)
        return carry

    lax.fori_loop(0, occ, own_gram, 0)

    def prepare_maps(p, carry):
        first_t[p] = maps_ref[p, 0].T
        second_maps[p, :, own_columns] = maps_ref[p, 1]
        return carry

    lax.fori_loop(0, pairs, prepare_maps, 0)

    def edge_step(d, e):
        region, valid, orbital = source(d, e)

        @pl.when(valid)
        def _():
            @pl.when(e >= slots)
            def _():
                edge_copy(d, e, orbital).wait_send()

            for i in range(occ):
                edge_gram[lax.rem(e, slots), i] = jnp.dot(
                    edge_t[i], far_rows[orbital], preferred_element_type=F32
                ).astype(BF16)
            edge_copy(d, e, orbital).start()

    def step(e, carry):
        for d in range(2):
            region, valid, orbital = source(d, e)
            is_gram = at_end[d] & (e >= occ)

            @pl.when(valid & jnp.logical_not(is_gram))
            def _(d=d, orbital=orbital):
                onward_copy(d, e - occ, orbital).wait_recv()
                rows_to_core(d, e, orbital, row_part).start()

                @pl.when(ahead_goes_on[d])
                def _():
                    onward_copy(d, e, orbital).start()

            @pl.when(valid & is_gram)
            def _(d=d, orbital=orbital):
                remote(
                    gram.at[orbital, :, gram_part],
                    gram.at[orbital, :, gram_part],
                    link_send.at[d, e],
                    link_recv.at[d, e],
                    sibling,
                ).wait_recv()
                gram_to_core(d, e, orbital, gram_part).start()

        for d in range(2):
            region, valid, orbital = source(d, e)
            is_gram = at_end[d] & (e >= occ)

            @pl.when(valid & jnp.logical_not(is_gram))
            def _(d=d, orbital=orbital):
                rows_to_core(d, e, orbital, row_rest).wait_recv()

                @pl.when(ahead_is_end[d] & (e >= occ))
                def _():
                    edge_step(d, e)

                for i in range(occ):
                    gram[orbital, i] = jnp.dot(
                        own_t[i], far_rows[orbital], preferred_element_type=F32
                    ).astype(BF16)

            @pl.when(valid & is_gram)
            def _(d=d, orbital=orbital):
                gram_to_core(d, e, orbital, gram_rest).wait_recv()

        for d in range(2):

            @pl.when(ahead_is_end[d] & (e == occ - 1))
            def _(d=d):
                for o in range(occ):
                    edge_t[o] = far_rows[ahead[d] * occ + o].T

                def first_edges(k, inner):
                    edge_step(d, k)
                    return inner

                lax.fori_loop(0, occ, first_edges, 0)

        return carry

    lax.fori_loop(0, steps, step, 0)

    remote(
        maps_ref.at[:, 1],
        second_maps.at[:, :, pl.ds(pl.multiple_of((1 - core) * columns, columns), columns)],
        maps_send,
        maps_recv,
        sibling,
    ).wait_recv()

    def peer_copy(k, c):
        block = pl.ds(c * CHUNK, CHUNK)
        return remote(
            partials.at[mine, block],
            partials.at[mine, block],
            peer_send.at[k - 1, c],
            peer_recv.at[k - 1, c],
            {"aux": lax.rem(mine + k, peers)},
        )

    def project(c, carry):
        for q in range(CHUNK):
            p = c * CHUNK + q
            matrix = gram[partner_ref[p], first_ref[p]]
            turned = jnp.dot(first_t[p], matrix, preferred_element_type=F32).astype(BF16)
            block = jnp.dot(turned, second_maps[p], preferred_element_type=F32)
            partials[mine, p] = block.astype(BF16)
        for k in range(1, peers):
            peer_copy(k, c).start()
        return carry

    lax.fori_loop(0, pairs // CHUNK, project, 0)

    def drain(e, carry):
        for d in range(2):
            region, valid, orbital = source(d, e)
            is_gram = at_end[d] & (e >= occ)

            @pl.when(valid & jnp.logical_not(is_gram))
            def _(d=d, orbital=orbital):
                rows_to_core(d, e, orbital, row_part).wait_send()

                @pl.when(ahead_goes_on[d])
                def _():
                    onward_copy(d, e, orbital).wait_send()

                @pl.when(
                    ahead_is_end[d] & ((e >= (regions - 2) * occ - slots))
                )
                def _():
                    edge_copy(d, e, orbital).wait_send()

            @pl.when(valid & is_gram)
            def _(d=d, orbital=orbital):
                gram_to_core(d, e, orbital, gram_part).wait_send()

        return carry

    lax.fori_loop(0, steps, drain, 0)
    for d in range(2):

        @pl.when(ahead_exists[d])
        def _(d=d):
            for o in range(occ):
                own_copy(d, o).wait_send()

    maps_copy().wait_send()

    def collect(c, carry):
        for k in range(1, peers):
            origin = lax.rem(mine - k + peers, peers)
            block = pl.ds(c * CHUNK, CHUNK)
            peer_copy(k, c).wait_send()
            remote(
                partials.at[origin, block],
                partials.at[origin, block],
                peer_send.at[k - 1, c],
                peer_recv.at[k - 1, c],
                {"aux": lax.rem(mine + k, peers)},
            ).wait_recv()
        for q in range(CHUNK):
            p = c * CHUNK + q
            total = partials[0, p].astype(F32)
            for k in range(1, peers):
                total = total + partials[k, p].astype(F32)
            out_ref[p] = total
        return carry

    lax.fori_loop(0, pairs // CHUNK, collect, 0)


def exchange_call(three_index, pno_maps, first_local, partner):
    regions = lax.axis_size("region")
    peers = lax.axis_size("aux")
    occ, aux_rows, virtuals = three_index.shape
    pairs, _, _, columns = pno_maps.shape
    width = columns * lax.axis_size("pno")
    orbitals = regions * occ
    steps = (regions - 1) * occ
    smem = pl.BlockSpec(memory_space=pltpu.SMEM)
    vmem = pl.BlockSpec(memory_space=pltpu.VMEM)
    dma = pltpu.SemaphoreType.DMA
    return pl.pallas_call(
        functools.partial(exchange_kernel, regions, peers),
        out_shape=jax.ShapeDtypeStruct((pairs, columns, width), F32),
        in_specs=[smem, smem, vmem, vmem],
        out_specs=vmem,
        scratch_shapes=[
            pltpu.VMEM((occ, virtuals, aux_rows), BF16),
            pltpu.VMEM((occ, virtuals, aux_rows), BF16),
            pltpu.VMEM((orbitals, aux_rows, virtuals), BF16),
            pltpu.VMEM((orbitals, occ, virtuals, virtuals), BF16),
            pltpu.VMEM((2 * occ, occ, virtuals, virtuals), BF16),
            pltpu.VMEM((pairs, virtuals, width), BF16),
            pltpu.VMEM((pairs, columns, virtuals), BF16),
            pltpu.VMEM((peers, pairs, columns, width), BF16),
            dma((2, steps)),
            dma((2, steps)),
            dma((2, steps)),
            dma((2, steps)),
            dma((2 * occ,)),
            dma,
            dma,
            dma((peers - 1, pairs // CHUNK)),
            dma((peers - 1, pairs // CHUNK)),
        ],
        compiler_params=pltpu.CompilerParams(
            collective_id=0, has_side_effects=True, vmem_limit_bytes=58 * 2**20
        ),
        cost_estimate=pl.CostEstimate(
            flops=10**10, bytes_accessed=150 * 10**6, transcendentals=0
        ),
        name="exchange",
    )(first_local, partner, three_index, pno_maps)


def update_kernel(
    near_ref,
    couplings_ref,
    occupied_ref,
    counts_ref,
    first_ref,
    partner_ref,
    start_ref,
    exchange_ref,
    below_ref,
    own_ref,
    above_ref,
    own_energies_ref,
    energies_ref,
    maps_ref,
    new_ref,
    density_ref,
    nearby,
    sems,
):
    pairs, columns, width = exchange_ref.shape
    copies = [
        pltpu.make_async_copy(ref, nearby.at[pl.ds(k * pairs, pairs)], sems.at[k])
        for k, ref in enumerate((below_ref, own_ref, above_ref))
    ]
    for copy in copies:
        copy.start()
    density_ref[...] = jnp.zeros_like(density_ref)
    start = start_ref[0]
    row_ids = start + lax.broadcasted_iota(jnp.int32, (columns, width), 0)
    col_ids = lax.broadcasted_iota(jnp.int32, (columns, width), 1)
    last_ids = jnp.maximum(row_ids, col_ids)
    for copy in copies:
        copy.wait()

    def one(p, carry):
        coupling = jnp.zeros((columns, width), F32)
        for n in range(near_ref.shape[1]):
            coupling = coupling + couplings_ref[p, n] * nearby[near_ref[p, n]].astype(F32)
        row_energy = jnp.broadcast_to(own_energies_ref[pl.ds(p, 1)], (width, columns)).T
        denominator = row_energy + energies_ref[pl.ds(p, 1)] - occupied_ref[p]
        update = jnp.where(
            last_ids < counts_ref[p], (coupling - exchange_ref[p]) / denominator, 0.0
        )
        new_ref[p] = update.astype(BF16)
        weight = jnp.sum(update * update, axis=1, keepdims=True) / width
        weight = jnp.broadcast_to(weight, (columns, columns)).T[0:8].astype(BF16)
        contract = (((1,), (1,)), ((), ()))
        for which, orbital in ((0, first_ref[p]), (1, partner_ref[p])):
            vec = lax.dot_general(
                weight, maps_ref[p, which], contract, preferred_element_type=F32
            )
            density_ref[pl.ds(orbital, 1)] += vec[0:1]
        return carry

    lax.fori_loop(0, pairs, one, 0)


def body(
    three_index,
    pno_maps,
    amplitudes,
    pair_orbitals,
    neighbours,
    couplings,
    pno_energies,
    occ_energies,
    pno_counts,
):
    regions = lax.axis_size("region")
    region_index = lax.axis_index("region")
    pno_index = lax.axis_index("pno")
    occ_dev, aux_rows, virtuals = three_index.shape
    pair_dev, _, _, columns = pno_maps.shape
    width = amplitudes.shape[2]
    mine = lax.dynamic_slice_in_dim(pair_orbitals, region_index * pair_dev, pair_dev)
    first_orb, partner = mine[:, 0], mine[:, 1]
    forward = [(i, i + 1) for i in range(regions - 1)]
    backward = [(target, origin) for origin, target in forward]
    below = lax.ppermute(amplitudes, "region", forward)
    above = lax.ppermute(amplitudes, "region", backward)
    exchange = exchange_call(three_index, pno_maps, first_orb - region_index * occ_dev, partner)
    near = neighbours - (region_index - 1) * pair_dev
    own_energies = lax.dynamic_slice_in_dim(pno_energies, pno_index * columns, columns, 1)
    occupied = jnp.take(occ_energies, first_orb) + jnp.take(occ_energies, partner)
    smem = pl.BlockSpec(memory_space=pltpu.SMEM)
    vmem = pl.BlockSpec(memory_space=pltpu.VMEM)
    anywhere = pl.BlockSpec(memory_space=pl.ANY)
    update, density = pl.pallas_call(
        update_kernel,
        out_shape=(
            jax.ShapeDtypeStruct((pair_dev, columns, width), BF16),
            jax.ShapeDtypeStruct((regions * occ_dev, virtuals), F32),
        ),
        in_specs=[smem] * 7 + [vmem] + [anywhere] * 3 + [vmem] * 3,
        out_specs=(vmem, vmem),
        scratch_shapes=[
            pltpu.VMEM((3 * pair_dev, columns, width), BF16),
            pltpu.SemaphoreType.DMA((3,)),
        ],
        compiler_params=pltpu.CompilerParams(vmem_limit_bytes=40 * 2**20),
        name="update",
    )(
        near,
        couplings,
        occupied,
        pno_counts,
        first_orb,
        partner,
        (pno_index * columns).reshape(1).astype(jnp.int32),
        exchange,
        below,
        amplitudes,
        above,
        own_energies,
        pno_energies,
        pno_maps,
    )
    density = lax.psum(density, ("region", "pno"))
    density = lax.dynamic_slice_in_dim(density, region_index * occ_dev, occ_dev)
    return (update, density)


def solution(mesh):
    in_specs = (
        P(("parts", "region"), "aux", None),
        P(("parts", "region"), None, None, "pno"),
        P(("parts", "region"), "pno", None),
        P("parts", None),
        P(("parts", "region"), None),
        P(("parts", "region"), None),
        P(("parts", "region"), None),
        P("parts"),
        P(("parts", "region")),
    )
    out_specs = (P(("parts", "region"), "pno", None), P(("parts", "region"), None))
    return jax.shard_map(body, mesh=mesh, in_specs=in_specs, out_specs=out_specs, check_vma=False)
```

time: 210 us -> 155 us (0.74)
  waiting for transfers between devices: 118 us -> 0.01 us
  Pallas kernels: 0 us -> 113 us
  local copies, waits for them, and re-layouts: 40.4 us -> 7.65 us
  blocking collectives: 3.03 us -> 26.5 us
  matrix products: 15 us -> 0 us
  between operations: 14 us -> 0.77 us
  other arithmetic: 10.4 us -> 0.53 us
    pallas_call x0 -> x2, Pallas kernels: none -> 113 us  [the longest x1 106 us: exchange_call(): pl.pallas_call(functools.partial(exchange_kernel, regions, peers), out_sh...]
    all_gather x2 -> x0, waiting for transfers between devices: 87.3 us -> none  [the longest x1 87.3 us: body(): all_rows = lax.all_gather(own_rows, 'region', axis=0, tiled=True)]
    psum x1, blocking collectives: 3.03 us -> 26.5 us  [body(): density = lax.psum(density, ('region', 'pno'))]
    gather x8 -> x2, local copies, waits for them, and re-layouts: 19.5 us -> 2.63 us  [the longest x1 1.32 us: body(): jnp.take(occ_energies, first_orb) + jnp.take(occ_energies, partner)]
    dot_general x6 -> x0, matrix products: 15 us -> none  [the longest x1 7.84 us: body(): jnp.einsum('ikv,jkw->ijvw', own_rows, all_rows, preferred_element_type=jn...]
    ppermute x2, waiting for transfers between devices: 13.5 us -> 0.01 us  [the longest x1 0.01 us: body(): below = lax.ppermute(amplitudes, 'region', forward)]
    psum x1 -> x0, waiting for transfers between devices: 8.96 us -> none  [body(): lax.psum(partial_exchange.astype(jnp.bfloat16), 'aux').astype(jnp.float32)]
    convert_element_type x1 -> x0, local copies, waits for them, and re-layouts: 6.89 us -> none  [body(): gram = gram.astype(jnp.bfloat16).reshape(-1, virtuals, virtuals)]
  transfers between devices with their start and end apart: 7 -> 2, of which waited for: 6 -> 0; matrix products, arithmetic and copies ran while one was open for 23% -> 4% of each run, Pallas kernels for 0% -> 68%
where the time goes in v2:
time: 155 us
  Pallas kernels  113 us (73%)
  blocking collectives  26.5 us (17%)
  local copies, waits for them, and re-layouts  7.65 us (5%)
  starting transfers between devices  6.29 us (4%)
    pallas_call x1, Pallas kernels, exchange_call(): pl.pallas_call(functools.partial(exchange_kernel, regions, peers), out_sh...  106 us
    psum x1, blocking collectives, body(): density = lax.psum(density, ('region', 'pno'))  26.5 us
    pallas_call x1, Pallas kernels, body(): pl.pallas_call(update_kernel, out_shape=(jax.ShapeDtypeStruct((pair_dev,...  7.48 us
    ppermute x1, starting transfers between devices, body(): below = lax.ppermute(amplitudes, 'region', forward)  5 us
    unnamed x16, local copies, waits for them, and re-layouts  3.13 us
  transfers between devices with their start and end apart: 2, of which 0 were waited for; matrix products, arithmetic and copies ran while one was open for 4% of the time, Pallas kernels for 68%

profile of v2, /device:TPU:0, one launch (start us, length us, event | category | flops | bytes accessed | tf_op | source)
XLA Modules:
  0.0 155.0 jit_solution(6688913672340808704)
XLA Ops:
  0.6 0.0 copy-start
  0.6 5.0 %collective-permute-start = (bf16[16,128,256]{2,1,0:T(8,128)(2,1)}, bf16[16,128,256]{2,1,0:T(8,128)(2,1)S(1)}, u32[]{:S(2)}, u32[]{:S(2)}) collective-permute-start(bf16[16,128,256]{2,1,0:T(8,128)(2,1)} %own_ref.1), channel_id=1, source_target_pairs={{0,4},{4,8},{8,12},{1,5},{5,9},{9,13},{2,6},{6,10},{10,14},{3,7},{... | collective-permute-start | bytes 3145736 | tf_op jit(solution)/shard_map/ppermute | solution.py:470
  5.6 1.3 collective-permute-start.1
  7.0 0.0 copy-done
  7.0 0.1 constant_dynamic-slice_fusion.2
  7.0 0.5 broadcast_subtract_fusion.1
  7.6 0.5 slice_bitcast_fusion
  8.1 0.8 copy.15
  8.8 0.8 copy.17.couplings_ref
  9.6 1.3 gather_fusion.1
  10.9 1.3 gather_fusion
  12.2 0.7 constant_dynamic-slice_fusion.1.own_energies_ref
  13.0 0.0 copy-start.1
  13.0 0.0 copy-start.3
  13.0 0.0 copy-start.4
  13.0 0.0 copy-start.5
  13.0 0.0 copy-start.6
  13.0 105.8 %exchange.1.exchange_ref = f32[16,128,256]{2,1,0:T(8,128)} custom-call(s32[16]{0:T(128)} %get-tuple-element.7.first_ref, s32[16]{0:T(128)} %get-tuple-element.10.partner_ref, bf16[3,1536,256]{2,1,0:T(8,128)(2,1)} %rows_ref.1, bf16[16,2,256,128]{3,2,1,0:T(8,128)(2,1)} %maps_ref.3), custom_call_target="tpu_custom_call" | custom-call | flops 10000000000 | bytes 150000000 | tf_op jit(solution)/shard_map/exchange/pallas_call | solution.py:357
  118.8 0.0 collective-permute-done.below_ref
  118.8 0.0 collective-permute-done.1.above_ref
  118.8 0.0 copy-done.1
  118.8 0.0 copy-done.3
  118.8 0.0 copy-done.4
  118.8 0.0 copy-done.5
  118.8 0.0 copy-done.6
  118.9 0.0 copy-start.2
  118.9 1.6 %copy-done.2 = f32[16,128,256]{2,1,0:T(8,128)S(1)} copy-done((f32[16,128,256]{2,1,0:T(8,128)S(1)}, f32[16,128,256]{2,1,0:T(8,128)}, u32[]{:S(2)}) %copy-start.2) | copy-done | bytes 2097176
  120.5 7.5 %update.1 = (bf16[16,128,256]{2,1,0:T(8,128)(2,1)}, f32[12,256]{1,0:T(8,128)S(1)}) custom-call(s32[16,4]{1,0:T(8,128)S(1)} %broadcast_subtract_fusion.near_ref, f32[16,4]{1,0:T(8,128)S(1)} %copy.17.couplings_ref, f32[16]{0:T(128)S(1)} %fusion.occupied_ref, s32[16]{0:T(128)S(1)} %copy-done.6, s32[16]{0:T(128)S(1)} %get-tuple-element.11.first_ref, ...), custom_call_target="tpu_custom_call" | custom-call | tf_op jit(solution)/shard_map/update/pallas_call | solution.py:479
  127.9 26.5 %psum.7 = f32[12,256]{1,0:T(8,128)S(1)} all-reduce(f32[12,256]{1,0:T(8,128)S(1)} %get-tuple-element.6), channel_id=1, replica_groups=mesh['parts'=2,'region'=4,'aux'=2,'pno'=2] {'region','pno'}, use_global_device_ids=true, to_apply=%region_0.0 | all-reduce | flops 3072 | bytes 24576 | tf_op jit(solution)/shard_map/psum | solution.py:509
  154.4 0.6 constant_dynamic-slice_fusion
  (3 shorter events, 0.0 us)
Async XLA Ops:
  0.6 6.3 %copy-start = (s32[64,2]{0,1:T(2,128)S(1)}, s32[64,2]{0,1:T(2,128)}, u32[]{:S(2)}) copy-start(s32[64,2]{0,1:T(2,128)} %param.14) | copy-start | bytes 1540
  0.6 118.1 %collective-permute-start = (bf16[16,128,256]{2,1,0:T(8,128)(2,1)}, bf16[16,128,256]{2,1,0:T(8,128)(2,1)S(1)}, u32[]{:S(2)}, u32[]{:S(2)}) collective-permute-start(bf16[16,128,256]{2,1,0:T(8,128)(2,1)} %own_ref.1), channel_id=1, source_target_pairs={{0,4},{4,8},{8,12},{1,5},{5,9},{9,13},{2,6},{6,10},{10,14},{3,7},{... | collective-permute-start | bytes 3145736 | tf_op jit(solution)/shard_map/ppermute | solution.py:470
  5.6 113.2 %collective-permute-start.1 = (bf16[16,128,256]{2,1,0:T(8,128)(2,1)}, bf16[16,128,256]{2,1,0:T(8,128)(2,1)S(1)}, u32[]{:S(2)}, u32[]{:S(2)}) collective-permute-start(bf16[16,128,256]{2,1,0:T(8,128)(2,1)} %own_ref.1), channel_id=1, source_target_pairs={{4,0},{8,4},{12,8},{5,1},{9,5},{13,9},{6,2},{10,6},{14,10},{7,3},{... | collective-permute-start | bytes 3145736 | tf_op jit(solution)/shard_map/ppermute | solution.py:471
  13.0 105.9 %copy-start.1 = (bf16[16,2,256,128]{3,2,1,0:T(8,128)(2,1)S(1)}, bf16[16,2,256,128]{3,2,1,0:T(8,128)(2,1)}, u32[]{:S(2)}) copy-start(bf16[16,2,256,128]{3,2,1,0:T(8,128)(2,1)} %maps_ref.3) | copy-start | bytes 6291460
  13.0 105.9 %copy-start.3 = (bf16[16,128,256]{2,1,0:T(8,128)(2,1)S(1)}, bf16[16,128,256]{2,1,0:T(8,128)(2,1)}, u32[]{:S(2)}) copy-start(bf16[16,128,256]{2,1,0:T(8,128)(2,1)} %own_ref.1) | copy-start | bytes 3145732
  13.0 105.9 %copy-start.4 = (f32[16,256]{1,0:T(8,128)S(1)}, f32[16,256]{1,0:T(8,128)}, u32[]{:S(2)}) copy-start(f32[16,256]{1,0:T(8,128)} %energies_ref.1) | copy-start | bytes 49156
  13.0 105.9 %copy-start.5 = (s32[16]{0:T(128)S(1)}, s32[16]{0:T(128)}, u32[]{:S(2)}) copy-start(s32[16]{0:T(128)} %get-tuple-element.10.partner_ref) | copy-start | bytes 196
  13.0 105.9 %copy-start.6 = (s32[16]{0:T(128)S(1)}, s32[16]{0:T(128)}, u32[]{:S(2)}) copy-start(s32[16]{0:T(128)} %counts_ref.1) | copy-start | bytes 196
  118.9 1.6 %copy-start.2 = (f32[16,128,256]{2,1,0:T(8,128)S(1)}, f32[16,128,256]{2,1,0:T(8,128)}, u32[]{:S(2)}) copy-start(f32[16,128,256]{2,1,0:T(8,128)} %exchange.1.exchange_ref) | copy-start | bytes 6291460

commit v3 on v2

v3 whole, which is shorter than its diff:
```python
import functools

import jax
import jax.numpy as jnp
from jax import lax
from jax.experimental import pallas as pl
from jax.experimental.pallas import tpu as pltpu
from jax.sharding import PartitionSpec as P

MESH = pl.DeviceIdType.MESH
F32 = jnp.float32
BF16 = jnp.bfloat16
CHUNK = 4


def exchange_kernel(
    regions,
    peers,
    orbitals_ref,
    near_ref,
    couplings_ref,
    occupied_ref,
    counts_ref,
    rows_ref,
    maps_ref,
    energies_ref,
    amplitudes_ref,
    new_ref,
    density_ref,
    own_t,
    edge_t,
    far_rows,
    gram,
    edge_gram,
    second_maps,
    first_t,
    partials,
    nearby,
    spread,
    gathered,
    link_send,
    link_recv,
    core_send,
    core_recv,
    edge_send,
    maps_send,
    maps_recv,
    peer_send,
    peer_recv,
    own_sem,
    halo_send,
    halo_recv,
    share_send,
    share_recv,
    spread_send,
    spread_recv,
):
    occ, aux_rows, virtuals = rows_ref.shape
    pairs = maps_ref.shape[0]
    columns = maps_ref.shape[3]
    z = lax.axis_index("region")
    core = lax.axis_index("pno")
    mine = lax.axis_index("aux")
    part = aux_rows // 2
    half = virtuals // 2
    steps = (regions - 1) * occ
    slots = 2 * occ
    row_part = pl.ds(pl.multiple_of(core * part, part), part)
    row_rest = pl.ds(pl.multiple_of((1 - core) * part, part), part)
    gram_part = pl.ds(pl.multiple_of(core * half, half), half)
    gram_rest = pl.ds(pl.multiple_of((1 - core) * half, half), half)
    own_columns = pl.ds(pl.multiple_of(core * columns, columns), columns)
    sibling = {"pno": 1 - core}

    members = 2 * regions
    place = 2 * z + core
    share = pairs // peers
    width = 2 * columns

    barrier = pltpu.get_barrier_semaphore()
    for k in range(1, members):
        target = lax.rem(place + k, members)
        pl.semaphore_signal(
            barrier,
            inc=1,
            device_id={"region": target // 2, "pno": lax.rem(target, 2)},
            device_id_type=MESH,
        )
    for k in range(1, peers):
        pl.semaphore_signal(
            barrier, inc=1, device_id={"aux": lax.rem(mine + k, peers)}, device_id_type=MESH
        )
    own_amplitudes = pltpu.make_async_copy(
        amplitudes_ref, nearby.at[pl.ds(pairs, pairs)], own_sem
    )
    own_amplitudes.start()
    pl.semaphore_wait(barrier, members - 1 + peers - 1)

    def remote(src, dst, send, recv, device):
        return pltpu.make_async_remote_copy(
            src_ref=src,
            dst_ref=dst,
            send_sem=send,
            recv_sem=recv,
            device_id=device,
            device_id_type=MESH,
        )

    ahead = (z + 1, z - 1)
    ahead_exists = (z < regions - 1, z > 0)
    ahead_is_end = (z == regions - 2, z == 1)
    ahead_goes_on = (z < regions - 2, z > 1)
    at_end = (z == regions - 1, z == 0)

    def source(d, e):
        region = z - 1 - e // occ if d == 0 else z + 1 + e // occ
        return region, (region >= 0) & (region < regions), region * occ + lax.rem(e, occ)

    def own_copy(d, o):
        return remote(
            rows_ref.at[o, row_part],
            far_rows.at[z * occ + o, row_part],
            link_send.at[d, o],
            link_recv.at[d, o],
            {"region": ahead[d]},
        )

    def onward_copy(d, e, orbital):
        return remote(
            far_rows.at[orbital, row_part],
            far_rows.at[orbital, row_part],
            link_send.at[d, e + occ],
            link_recv.at[d, e + occ],
            {"region": ahead[d]},
        )

    def rows_to_core(d, e, orbital, which):
        return remote(
            far_rows.at[orbital, which],
            far_rows.at[orbital, which],
            core_send.at[d, e],
            core_recv.at[d, e],
            sibling,
        )

    def gram_to_core(d, e, orbital, which):
        return remote(
            gram.at[orbital, :, which],
            gram.at[orbital, :, which],
            core_send.at[d, e],
            core_recv.at[d, e],
            sibling,
        )

    def edge_copy(d, e, orbital):
        slot = lax.rem(e, slots)
        return remote(
            edge_gram.at[slot, :, gram_part],
            gram.at[orbital, :, gram_part],
            edge_send.at[slot],
            link_recv.at[d, e + occ],
            {"region": ahead[d]},
        )

    def maps_copy():
        return remote(
            maps_ref.at[:, 1],
            second_maps.at[:, :, own_columns],
            maps_send,
            maps_recv,
            sibling,
        )

    def halo_copy(d):
        return remote(
            nearby.at[pl.ds(pairs + mine * share, share)],
            nearby.at[pl.ds((0 if d == 0 else 2) * pairs + mine * share, share)],
            halo_send.at[d],
            halo_recv.at[d],
            {"region": ahead[d]},
        )

    def share_copy(d, k, origin):
        block = nearby.at[pl.ds((0 if d == 0 else 2) * pairs + origin * share, share)]
        return remote(
            block,
            block,
            share_send.at[d, k - 1],
            share_recv.at[d, k - 1],
            {"aux": lax.rem(mine + k, peers)},
        )

    behind_exists = (z > 0, z < regions - 1)

    for d in range(2):

        @pl.when(ahead_exists[d])
        def _(d=d):
            for o in range(occ):
                own_copy(d, o).start()

        @pl.when(jnp.logical_not(behind_exists[d]))
        def _(d=d):
            nearby[pl.ds((0 if d == 0 else 2) * pairs, pairs)] = jnp.zeros(
                (pairs, columns, width), BF16
            )

    maps_copy().start()
    for o in range(occ):
        own_t[o] = rows_ref[o].T

    def own_gram(o, carry):
        for i in range(occ):
            gram[z * occ + o, i] = jnp.dot(
                own_t[i], rows_ref[o], preferred_element_type=F32
            ).astype(BF16)
        return carry

    lax.fori_loop(0, occ, own_gram, 0)

    def prepare_maps(p, carry):
        first_t[p] = maps_ref[p, 0].T
        second_maps[p, :, own_columns] = maps_ref[p, 1]
        return carry

    lax.fori_loop(0, pairs, prepare_maps, 0)
    own_amplitudes.wait()

    def edge_step(d, e):
        region, valid, orbital = source(d, e)

        @pl.when(valid)
        def _():
            @pl.when(e >= slots)
            def _():
                edge_copy(d, e, orbital).wait_send()

            for i in range(occ):
                edge_gram[lax.rem(e, slots), i] = jnp.dot(
                    edge_t[i], far_rows[orbital], preferred_element_type=F32
                ).astype(BF16)
            edge_copy(d, e, orbital).start()

    def step(e, carry):
        for d in range(2):
            region, valid, orbital = source(d, e)
            is_gram = at_end[d] & (e >= occ)

            @pl.when(valid & jnp.logical_not(is_gram))
            def _(d=d, orbital=orbital):
                onward_copy(d, e - occ, orbital).wait_recv()
                rows_to_core(d, e, orbital, row_part).start()

                @pl.when(ahead_goes_on[d])
                def _():
                    onward_copy(d, e, orbital).start()

            @pl.when(valid & is_gram)
            def _(d=d, orbital=orbital):
                remote(
                    gram.at[orbital, :, gram_part],
                    gram.at[orbital, :, gram_part],
                    link_send.at[d, e],
                    link_recv.at[d, e],
                    sibling,
                ).wait_recv()
                gram_to_core(d, e, orbital, gram_part).start()

        for d in range(2):

            @pl.when(ahead_exists[d] & (e == occ))
            def _(d=d):
                halo_copy(d).start()

        for d in range(2):
            region, valid, orbital = source(d, e)
            is_gram = at_end[d] & (e >= occ)

            @pl.when(valid & jnp.logical_not(is_gram))
            def _(d=d, orbital=orbital):
                rows_to_core(d, e, orbital, row_rest).wait_recv()

                @pl.when(ahead_is_end[d] & (e >= occ))
                def _():
                    edge_step(d, e)

                for i in range(occ):
                    gram[orbital, i] = jnp.dot(
                        own_t[i], far_rows[orbital], preferred_element_type=F32
                    ).astype(BF16)

            @pl.when(valid & is_gram)
            def _(d=d, orbital=orbital):
                gram_to_core(d, e, orbital, gram_rest).wait_recv()

        for d in range(2):

            @pl.when(ahead_is_end[d] & (e == occ - 1))
            def _(d=d):
                for o in range(occ):
                    edge_t[o] = far_rows[ahead[d] * occ + o].T

                def first_edges(k, inner):
                    edge_step(d, k)
                    return inner

                lax.fori_loop(0, occ, first_edges, 0)

        return carry

    lax.fori_loop(0, steps, step, 0)

    remote(
        maps_ref.at[:, 1],
        second_maps.at[:, :, pl.ds(pl.multiple_of((1 - core) * columns, columns), columns)],
        maps_send,
        maps_recv,
        sibling,
    ).wait_recv()

    def peer_copy(k, c):
        block = pl.ds(c * CHUNK, CHUNK)
        return remote(
            partials.at[mine, block],
            partials.at[mine, block],
            peer_send.at[k - 1, c],
            peer_recv.at[k - 1, c],
            {"aux": lax.rem(mine + k, peers)},
        )

    def project(c, carry):
        for q in range(CHUNK):
            p = c * CHUNK + q
            first = jnp.clip(orbitals_ref[z * pairs + p, 0] - z * occ, 0, occ - 1)
            matrix = gram[orbitals_ref[z * pairs + p, 1], first]
            turned = jnp.dot(first_t[p], matrix, preferred_element_type=F32).astype(BF16)
            block = jnp.dot(turned, second_maps[p], preferred_element_type=F32)
            partials[mine, p] = block.astype(BF16)
        for k in range(1, peers):
            peer_copy(k, c).start()
        return carry

    lax.fori_loop(0, pairs // CHUNK, project, 0)

    for d in range(2):

        @pl.when(behind_exists[d])
        def _(d=d):
            block = nearby.at[pl.ds((0 if d == 0 else 2) * pairs + mine * share, share)]
            remote(block, block, halo_send.at[d], halo_recv.at[d], sibling).wait_recv()
            for k in range(1, peers):
                share_copy(d, k, mine).start()

    for d in range(2):

        @pl.when(behind_exists[d])
        def _(d=d):
            for k in range(1, peers):
                share_copy(d, k, mine).wait_send()
                share_copy(d, k, lax.rem(mine - k + peers, peers)).wait_recv()

    row_ids = core * columns + lax.broadcasted_iota(jnp.int32, (columns, width), 0)
    col_ids = lax.broadcasted_iota(jnp.int32, (columns, width), 1)
    last_ids = jnp.maximum(row_ids, col_ids)
    orbital_ids = lax.broadcasted_iota(
        jnp.int32, spread.shape, 0
    ) * occ + lax.broadcasted_iota(jnp.int32, spread.shape, 1)
    held = lax.broadcasted_iota(jnp.int32, spread.shape, 1) < occ
    orbital_ids = jnp.where(held, orbital_ids, -1)
    spread[...] = jnp.zeros_like(spread)
    contract = (((1,), (1,)), ((), ()))

    def collect(c, carry):
        for k in range(1, peers):
            origin = lax.rem(mine - k + peers, peers)
            block = pl.ds(c * CHUNK, CHUNK)
            remote(
                partials.at[origin, block],
                partials.at[origin, block],
                peer_send.at[k - 1, c],
                peer_recv.at[k - 1, c],
                {"aux": lax.rem(mine + k, peers)},
            ).wait_recv()
        for q in range(CHUNK):
            p = c * CHUNK + q
            exchange = partials[0, p].astype(F32)
            for k in range(1, peers):
                exchange = exchange + partials[k, p].astype(F32)
            coupling = jnp.zeros((columns, width), F32)
            for n in range(near_ref.shape[1]):
                taken = nearby[jnp.clip(near_ref[p, n] - (z - 1) * pairs, 0, 3 * pairs - 1)]
                coupling = coupling + couplings_ref[p, n] * taken.astype(F32)
            first = orbitals_ref[z * pairs + p, 0]
            second = orbitals_ref[z * pairs + p, 1]
            occupied = occupied_ref[first] + occupied_ref[second]
            energies = energies_ref[pl.ds(p, 1)]
            own_energies = jnp.where(core == 0, energies[:, :columns], energies[:, columns:])
            row_energy = jnp.broadcast_to(own_energies, (width, columns)).T
            denominator = row_energy + energies - occupied
            update = jnp.where(
                last_ids < counts_ref[p], (coupling - exchange) / denominator, 0.0
            )
            new_ref[p] = update.astype(BF16)
            weight = jnp.sum(update * update, axis=1, keepdims=True) / width
            weight = jnp.broadcast_to(weight, (columns, columns)).T[0:8].astype(BF16)
            for which, orbital in ((0, first), (1, second)):
                vec = lax.dot_general(
                    weight, maps_ref[p, which], contract, preferred_element_type=F32
                )
                spread[...] += jnp.where(orbital_ids == orbital, vec[None], 0.0)
        return carry

    lax.fori_loop(0, pairs // CHUNK, collect, 0)

    def spread_copy(k):
        target = lax.rem(place + k, members)
        return remote(
            spread.at[target // 2],
            gathered.at[place],
            spread_send.at[k - 1],
            spread_recv.at[k - 1],
            {"region": target // 2, "pno": lax.rem(target, 2)},
        )

    for k in range(1, members):
        spread_copy(k).start()
    gathered[place] = spread[z]

    def drain(e, carry):
        for d in range(2):
            region, valid, orbital = source(d, e)
            is_gram = at_end[d] & (e >= occ)

            @pl.when(valid & jnp.logical_not(is_gram))
            def _(d=d, orbital=orbital):
                rows_to_core(d, e, orbital, row_part).wait_send()

                @pl.when(ahead_goes_on[d])
                def _():
                    onward_copy(d, e, orbital).wait_send()

                @pl.when(
                    ahead_is_end[d] & ((e >= (regions - 2) * occ - slots))
                )
                def _():
                    edge_copy(d, e, orbital).wait_send()

            @pl.when(valid & is_gram)
            def _(d=d, orbital=orbital):
                gram_to_core(d, e, orbital, gram_part).wait_send()

        return carry

    lax.fori_loop(0, steps, drain, 0)
    for d in range(2):

        @pl.when(ahead_exists[d])
        def _(d=d):
            for o in range(occ):
                own_copy(d, o).wait_send()

    maps_copy().wait_send()

    for d in range(2):

        @pl.when(ahead_exists[d])
        def _(d=d):
            halo_copy(d).wait_send()

    def drain_peers(c, carry):
        for k in range(1, peers):
            peer_copy(k, c).wait_send()
        return carry

    lax.fori_loop(0, pairs // CHUNK, drain_peers, 0)
    for k in range(1, members):
        spread_copy(k).wait_send()
        origin = lax.rem(place - k + members, members)
        remote(
            gathered.at[origin],
            gathered.at[origin],
            spread_send.at[k - 1],
            spread_recv.at[k - 1],
            sibling,
        ).wait_recv()
    total = gathered[0]
    for k in range(1, members):
        total = total + gathered[k]
    density_ref[...] = total[0:occ]


def body(
    three_index,
    pno_maps,
    amplitudes,
    pair_orbitals,
    neighbours,
    couplings,
    pno_energies,
    occ_energies,
    pno_counts,
):
    regions = lax.axis_size("region")
    peers = lax.axis_size("aux")
    occ, aux_rows, virtuals = three_index.shape
    pairs, _, _, columns = pno_maps.shape
    width = columns * lax.axis_size("pno")
    orbitals = regions * occ
    steps = (regions - 1) * occ
    smem = pl.BlockSpec(memory_space=pltpu.SMEM)
    vmem = pl.BlockSpec(memory_space=pltpu.VMEM)
    anywhere = pl.BlockSpec(memory_space=pl.ANY)
    dma = pltpu.SemaphoreType.DMA
    return pl.pallas_call(
        functools.partial(exchange_kernel, regions, peers),
        out_shape=(
            jax.ShapeDtypeStruct((pairs, columns, width), BF16),
            jax.ShapeDtypeStruct((occ, virtuals), F32),
        ),
        in_specs=[smem] * 5 + [vmem] * 3 + [anywhere],
        out_specs=(vmem, vmem),
        scratch_shapes=[
            pltpu.VMEM((occ, virtuals, aux_rows), BF16),
            pltpu.VMEM((occ, virtuals, aux_rows), BF16),
            pltpu.VMEM((orbitals, aux_rows, virtuals), BF16),
            pltpu.VMEM((orbitals, occ, virtuals, virtuals), BF16),
            pltpu.VMEM((2 * occ, occ, virtuals, virtuals), BF16),
            pltpu.VMEM((pairs, virtuals, width), BF16),
            pltpu.VMEM((pairs, columns, virtuals), BF16),
            pltpu.VMEM((peers, pairs, columns, width), BF16),
            pltpu.VMEM((3 * pairs, columns, width), BF16),
            pltpu.VMEM((regions, 8, virtuals), F32),
            pltpu.VMEM((2 * regions, 8, virtuals), F32),
            dma((2, steps)),
            dma((2, steps)),
            dma((2, steps)),
            dma((2, steps)),
            dma((2 * occ,)),
            dma,
            dma,
            dma((peers - 1, pairs // CHUNK)),
            dma((peers - 1, pairs // CHUNK)),
            dma,
            dma((2,)),
            dma((2,)),
            dma((2, peers - 1)),
            dma((2, peers - 1)),
            dma((2 * regions - 1,)),
            dma((2 * regions - 1,)),
        ],
        compiler_params=pltpu.CompilerParams(
            collective_id=0, has_side_effects=True, vmem_limit_bytes=58 * 2**20
        ),
        cost_estimate=pl.CostEstimate(
            flops=10**10, bytes_accessed=150 * 10**6, transcendentals=0
        ),
        name="update",
    )(
        pair_orbitals,
        neighbours,
        couplings,
        occ_energies,
        pno_counts,
        three_index,
        pno_maps,
        pno_energies,
        amplitudes,
    )


def solution(mesh):
    in_specs = (
        P(("parts", "region"), "aux", None),
        P(("parts", "region"), None, None, "pno"),
        P(("parts", "region"), "pno", None),
        P("parts", None),
        P(("parts", "region"), None),
        P(("parts", "region"), None),
        P(("parts", "region"), None),
        P("parts"),
        P(("parts", "region")),
    )
    out_specs = (P(("parts", "region"), "pno", None), P(("parts", "region"), None))
    return jax.shard_map(body, mesh=mesh, in_specs=in_specs, out_specs=out_specs, check_vma=False)
```

time: 155 us -> 131 us (0.85)
  blocking collectives: 26.5 us -> 0 us
  Pallas kernels: 113 us -> 123 us
  starting transfers between devices: 6.29 us -> 0 us
    psum x1 -> x0, blocking collectives: 26.5 us -> none  [body(): density = lax.psum(density, ('region', 'pno'))]
    pallas_call x2 -> x1, Pallas kernels: 113 us -> 123 us  [body(): pl.pallas_call(functools.partial(exchange_kernel, regions, peers), out_sh...]
    ppermute x2 -> x0, starting transfers between devices: 6.29 us -> none  [the longest x1 5 us: body(): below = lax.ppermute(amplitudes, 'region', forward)]
    unnamed x16 -> x5, local copies, waits for them, and re-layouts: 3.13 us -> 7.64 us
    gather x2 -> x0, local copies, waits for them, and re-layouts: 2.63 us -> none  [the longest x1 1.32 us: body(): jnp.take(occ_energies, first_orb) + jnp.take(occ_energies, partner)]
  transfers between devices with their start and end apart: 2 -> 0, of which waited for: 0 -> 0; matrix products, arithmetic and copies ran while one was open for 4% -> 0% of each run, Pallas kernels for 68% -> 0%
where the time goes in v3:
time: 131 us
  Pallas kernels  123 us (94%)
  local copies, waits for them, and re-layouts  7.64 us (6%)
    pallas_call x1, Pallas kernels, body(): pl.pallas_call(functools.partial(exchange_kernel, regions, peers), out_sh...  123 us
    unnamed x5, local copies, waits for them, and re-layouts  7.64 us

profile of v3, /device:TPU:0, one launch (start us, length us, event | category | flops | bytes accessed | tf_op | source)
XLA Modules:
  0.0 131.2 jit_solution(11271252579611969423)
XLA Ops:
  0.6 1.4 %copy.12.near_ref = s32[16,4]{1,0:T(8,128)} copy(s32[16,4]{0,1:T(4,128)} %param.13) | data formatting | bytes 512 | tf_op args[4]
  2.0 1.3 %copy.13.couplings_ref = f32[16,4]{1,0:T(8,128)} copy(f32[16,4]{0,1:T(4,128)} %param.14) | data formatting | bytes 512 | tf_op args[5]
  3.3 1.4 %copy.11.orbitals_ref = s32[64,2]{1,0:T(8,128)} copy(s32[64,2]{0,1:T(2,128)} %param.12) | data formatting | bytes 1024 | tf_op args[3]
  4.7 122.9 %update.1 = (bf16[16,128,256]{2,1,0:T(8,128)(2,1)}, f32[3,256]{1,0:T(4,128)}) custom-call(s32[64,2]{1,0:T(8,128)} %copy.11.orbitals_ref, s32[16,4]{1,0:T(8,128)} %copy.12.near_ref, f32[16,4]{1,0:T(8,128)} %copy.13.couplings_ref, f32[12]{0:T(128)} %occupied_ref.1, s32[16]{0:T(128)} %counts_ref.1, bf16[3,1536,256]{2,1,0:T(8,128)(2,1)} %rows_ref.1, ...), custom_call_target="tpu_custom_call" | custom-call | flops 10000000000 | bytes 150000000 | tf_op jit(solution)/shard_map/update/pallas_call | solution.py:514
  127.6 2.3 %copy.16 = bf16[16,128,256]{2,1,0:T(8,128)(2,1)} copy(bf16[16,128,256]{2,1,0:T(8,128)(2,1)} %get-tuple-element.4) | data formatting | bytes 2097152
  129.9 1.3 copy.17

commit v4 on v3

--- a/solution.py
+++ b/solution.py
@@ -11,16 +11,18 @@
 F32 = jnp.float32
 BF16 = jnp.bfloat16
 CHUNK = 4
+DEPTH = 2
+HALO_STEP = 0
+SHARE_STEP = 2
 
 
 def exchange_kernel(
     regions,
     peers,
-    orbitals_ref,
-    near_ref,
-    couplings_ref,
+    whole_ref,
     occupied_ref,
     counts_ref,
+    couplings_ref,
     rows_ref,
     maps_ref,
     energies_ref,
@@ -196,7 +198,7 @@
 
         @pl.when(ahead_exists[d])
         def _(d=d):
-            for o in range(occ):
+            for o in range(DEPTH):
                 own_copy(d, o).start()
 
         @pl.when(jnp.logical_not(behind_exists[d]))
@@ -241,6 +243,21 @@
                 ).astype(BF16)
             edge_copy(d, e, orbital).start()
 
+    def in_queue(d, k, act):
+        @pl.when(ahead_exists[d] & (k < occ))
+        def _():
+            act(own_copy(d, k))
+
+        region, valid, orbital = source(d, k - occ)
+
+        @pl.when(ahead_goes_on[d] & valid & (k >= occ))
+        def _():
+            act(onward_copy(d, k - occ, orbital))
+
+    def queue_step(d, e):
+        in_queue(d, e, lambda copy: copy.wait_send())
+        in_queue(d, e + DEPTH, lambda copy: copy.start())
+
     def step(e, carry):
         for d in range(2):
             region, valid, orbital = source(d, e)
@@ -250,10 +267,6 @@
             def _(d=d, orbital=orbital):
                 onward_copy(d, e - occ, orbital).wait_recv()
                 rows_to_core(d, e, orbital, row_part).start()
-
-                @pl.when(ahead_goes_on[d])
-                def _():
-                    onward_copy(d, e, orbital).start()
 
             @pl.when(valid & is_gram)
             def _(d=d, orbital=orbital):
@@ -268,9 +281,18 @@
 
         for d in range(2):
 
-            @pl.when(ahead_exists[d] & (e == occ))
+            queue_step(d, e)
+
+            @pl.when(ahead_exists[d] & (e == HALO_STEP))
             def _(d=d):
                 halo_copy(d).start()
+
+            @pl.when(behind_exists[d] & (e == SHARE_STEP))
+            def _(d=d):
+                block = nearby.at[pl.ds((0 if d == 0 else 2) * pairs + mine * share, share)]
+                remote(block, block, halo_send.at[d], halo_recv.at[d], sibling).wait_recv()
+                for k in range(1, peers):
+                    share_copy(d, k, mine).start()
 
         for d in range(2):
             region, valid, orbital = source(d, e)
@@ -331,8 +353,8 @@
     def project(c, carry):
         for q in range(CHUNK):
             p = c * CHUNK + q
-            first = jnp.clip(orbitals_ref[z * pairs + p, 0] - z * occ, 0, occ - 1)
-            matrix = gram[orbitals_ref[z * pairs + p, 1], first]
+            first = jnp.clip(whole_ref[2 * p] - z * occ, 0, occ - 1)
+            matrix = gram[whole_ref[2 * p + 1], first]
             turned = jnp.dot(first_t[p], matrix, preferred_element_type=F32).astype(BF16)
             block = jnp.dot(turned, second_maps[p], preferred_element_type=F32)
             partials[mine, p] = block.astype(BF16)
@@ -341,15 +363,6 @@
         return carry
 
     lax.fori_loop(0, pairs // CHUNK, project, 0)
-
-    for d in range(2):
-
-        @pl.when(behind_exists[d])
-        def _(d=d):
-            block = nearby.at[pl.ds((0 if d == 0 else 2) * pairs + mine * share, share)]
-            remote(block, block, halo_send.at[d], halo_recv.at[d], sibling).wait_recv()
-            for k in range(1, peers):
-                share_copy(d, k, mine).start()
 
     for d in range(2):
 
@@ -387,11 +400,12 @@
             for k in range(1, peers):
                 exchange = exchange + partials[k, p].astype(F32)
             coupling = jnp.zeros((columns, width), F32)
-            for n in range(near_ref.shape[1]):
-                taken = nearby[jnp.clip(near_ref[p, n] - (z - 1) * pairs, 0, 3 * pairs - 1)]
-                coupling = coupling + couplings_ref[p, n] * taken.astype(F32)
-            first = orbitals_ref[z * pairs + p, 0]
-            second = orbitals_ref[z * pairs + p, 1]
+            factors = couplings_ref[pl.ds(p, 1)]
+            for n in range(couplings_ref.shape[1]):
+                taken = nearby[jnp.clip(whole_ref[(2 + n) * pairs + p] - (z - 1) * pairs, 0, 3 * pairs - 1)]
+                coupling = coupling + factors[:, n : n + 1] * taken.astype(F32)
+            first = whole_ref[2 * p]
+            second = whole_ref[2 * p + 1]
             occupied = occupied_ref[first] + occupied_ref[second]
             energies = energies_ref[pl.ds(p, 1)]
             own_energies = jnp.where(core == 0, energies[:, :columns], energies[:, columns:])
@@ -435,10 +449,6 @@
             def _(d=d, orbital=orbital):
                 rows_to_core(d, e, orbital, row_part).wait_send()
 
-                @pl.when(ahead_goes_on[d])
-                def _():
-                    onward_copy(d, e, orbital).wait_send()
-
                 @pl.when(
                     ahead_is_end[d] & ((e >= (regions - 2) * occ - slots))
                 )
@@ -452,13 +462,6 @@
         return carry
 
     lax.fori_loop(0, steps, drain, 0)
-    for d in range(2):
-
-        @pl.when(ahead_exists[d])
-        def _(d=d):
-            for o in range(occ):
-                own_copy(d, o).wait_send()
-
     maps_copy().wait_send()
 
     for d in range(2):
@@ -507,6 +510,8 @@
     width = columns * lax.axis_size("pno")
     orbitals = regions * occ
     steps = (regions - 1) * occ
+    mine = lax.dynamic_slice_in_dim(pair_orbitals, lax.axis_index("region") * pairs, pairs)
+    whole = jnp.concatenate([mine.reshape(-1), neighbours.T.reshape(-1)])
     smem = pl.BlockSpec(memory_space=pltpu.SMEM)
     vmem = pl.BlockSpec(memory_space=pltpu.VMEM)
     anywhere = pl.BlockSpec(memory_space=pl.ANY)
@@ -517,7 +522,7 @@
             jax.ShapeDtypeStruct((pairs, columns, width), BF16),
             jax.ShapeDtypeStruct((occ, virtuals), F32),
         ),
-        in_specs=[smem] * 5 + [vmem] * 3 + [anywhere],
+        in_specs=[smem] * 3 + [vmem] * 4 + [anywhere],
         out_specs=(vmem, vmem),
         scratch_shapes=[
             pltpu.VMEM((occ, virtuals, aux_rows), BF16),
@@ -556,11 +561,10 @@
         ),
         name="update",
     )(
-        pair_orbitals,
-        neighbours,
-        couplings,
+        whole,
         occ_energies,
         pno_counts,
+        couplings,
         three_index,
         pno_maps,
         pno_energies,

time: 131 us -> 120 us (0.916)
  Pallas kernels: 123 us -> 112 us
    pallas_call x1, Pallas kernels: 123 us -> 112 us  [body(): pl.pallas_call(functools.partial(exchange_kernel, regions, peers), out_sh...]
    unnamed x5, local copies, waits for them, and re-layouts: 7.64 us -> 5.58 us
where the time goes in v4:
time: 120 us
  Pallas kernels  112 us (93%)
  local copies, waits for them, and re-layouts  6.58 us (5%)
    pallas_call x1, Pallas kernels, body(): pl.pallas_call(functools.partial(exchange_kernel, regions, peers), out_sh...  112 us
    unnamed x5, local copies, waits for them, and re-layouts  5.58 us

profile of v4, /device:TPU:0, one launch (start us, length us, event | category | flops | bytes accessed | tf_op | source)
XLA Modules:
  0.0 119.8 jit_solution(18242809042282120538)
XLA Ops:
  0.6 0.0 copy-start
  0.6 0.7 copy-done
  1.3 0.1 constant_dynamic-slice_fusion
  1.4 0.8 reshape.11
  2.1 0.1 copy.13
  2.2 0.1 reshape.10
  2.3 0.6 pad_add_fusion.whole_ref
  2.9 1.4 %copy.14.couplings_ref = f32[16,4]{1,0:T(8,128)} copy(f32[16,4]{0,1:T(4,128)} %param.14) | data formatting | bytes 512 | tf_op args[5]
  4.3 112.0 %update.1 = (bf16[16,128,256]{2,1,0:T(8,128)(2,1)}, f32[3,256]{1,0:T(4,128)}) custom-call(s32[96]{0:T(128)} %pad_add_fusion.whole_ref, f32[12]{0:T(128)} %occupied_ref.1, s32[16]{0:T(128)} %counts_ref.1, f32[16,4]{1,0:T(8,128)} %copy.14.couplings_ref, bf16[3,1536,256]{2,1,0:T(8,128)(2,1)} %rows_ref.1, bf16[16,2,256,128]{3,2,1,0:T(8,128)(2,1)} %maps_ref.1, ...), custom_call_target="tpu_custom_call" | custom-call | flops 10000000000 | bytes 150000000 | tf_op jit(solution)/shard_map/update/pallas_call | solution.py:519
  116.3 2.3 %copy.17 = bf16[16,128,256]{2,1,0:T(8,128)(2,1)} copy(bf16[16,128,256]{2,1,0:T(8,128)(2,1)} %get-tuple-element.4) | data formatting | bytes 2097152
  118.6 1.3 %copy.18 = f32[3,256]{1,0:T(4,128)} copy(f32[3,256]{1,0:T(4,128)} %get-tuple-element.5) | data formatting | bytes 6144
Async XLA Ops:
  0.6 0.7 copy-start

commit v5 on v4

--- a/solution.py
+++ b/solution.py
@@ -12,8 +12,7 @@
 BF16 = jnp.bfloat16
 CHUNK = 4
 DEPTH = 2
-HALO_STEP = 0
-SHARE_STEP = 2
+SHARE_STEP = 1
 
 
 def exchange_kernel(
@@ -192,6 +191,7 @@
             {"aux": lax.rem(mine + k, peers)},
         )
 
+    own_amplitudes.wait()
     behind_exists = (z > 0, z < regions - 1)
 
     for d in range(2):
@@ -200,6 +200,7 @@
         def _(d=d):
             for o in range(DEPTH):
                 own_copy(d, o).start()
+            halo_copy(d).start()
 
         @pl.when(jnp.logical_not(behind_exists[d]))
         def _(d=d):
@@ -226,7 +227,6 @@
         return carry
 
     lax.fori_loop(0, pairs, prepare_maps, 0)
-    own_amplitudes.wait()
 
     def edge_step(d, e):
         region, valid, orbital = source(d, e)
@@ -282,10 +282,6 @@
         for d in range(2):
 
             queue_step(d, e)
-
-            @pl.when(ahead_exists[d] & (e == HALO_STEP))
-            def _(d=d):
-                halo_copy(d).start()
 
             @pl.when(behind_exists[d] & (e == SHARE_STEP))
             def _(d=d):

time: 120 us -> 120 us (level)
  no operation moved by 1% of the time
where the time goes in v5:
time: 120 us
  Pallas kernels  112 us (93%)
  local copies, waits for them, and re-layouts  6.58 us (5%)
    pallas_call x1, Pallas kernels, body(): pl.pallas_call(functools.partial(exchange_kernel, regions, peers), out_sh...  112 us
    unnamed x5, local copies, waits for them, and re-layouts  5.58 us

profile of v5, /device:TPU:0, one launch (start us, length us, event | category | flops | bytes accessed | tf_op | source)
XLA Modules:
  0.0 119.8 jit_solution(5229798601973744100)
XLA Ops:
  0.6 0.0 copy-start
  0.6 0.7 copy-done
  1.3 0.1 constant_dynamic-slice_fusion
  1.4 0.8 reshape.11
  2.1 0.1 copy.13
  2.2 0.1 reshape.10
  2.3 0.6 pad_add_fusion.whole_ref
  2.9 1.4 %copy.14.couplings_ref = f32[16,4]{1,0:T(8,128)} copy(f32[16,4]{0,1:T(4,128)} %param.14) | data formatting | bytes 512 | tf_op args[5]
  4.3 112.0 %update.1 = (bf16[16,128,256]{2,1,0:T(8,128)(2,1)}, f32[3,256]{1,0:T(4,128)}) custom-call(s32[96]{0:T(128)} %pad_add_fusion.whole_ref, f32[12]{0:T(128)} %occupied_ref.1, s32[16]{0:T(128)} %counts_ref.1, f32[16,4]{1,0:T(8,128)} %copy.14.couplings_ref, bf16[3,1536,256]{2,1,0:T(8,128)(2,1)} %rows_ref.1, bf16[16,2,256,128]{3,2,1,0:T(8,128)(2,1)} %maps_ref.1, ...), custom_call_target="tpu_custom_call" | custom-call | flops 10000000000 | bytes 150000000 | tf_op jit(solution)/shard_map/update/pallas_call | solution.py:515
  116.3 2.3 %copy.17 = bf16[16,128,256]{2,1,0:T(8,128)(2,1)} copy(bf16[16,128,256]{2,1,0:T(8,128)(2,1)} %get-tuple-element.4) | data formatting | bytes 2097152
  118.6 1.3 %copy.18 = f32[3,256]{1,0:T(4,128)} copy(f32[3,256]{1,0:T(4,128)} %get-tuple-element.5) | data formatting | bytes 6144
Async XLA Ops:
  0.6 0.7 copy-start
